TPU v7x, 32 devices: a whole 2x2x4 slice. The times are simulated.
32 devices in a mesh: gx: 4 (over y, core), gy: 8 (over z, x).
Axes of the slice: x: 2, y: 2, z: 4, core: 2. Of those that a mesh axis runs over, the one named last changes fastest.
Arguments:
- motion: float32 [384, 128, 3, 512], P('gx', 'gy'), may hold values from -40 to 40
- time_sketch: float32 [512, 128], replicated, may hold values from -0.25 to 0.25
- x_sketch: float32 [384, 128], replicated, may hold values from -0.3125 to 0.3125
Outputs:
- time_core: float32 [384, 128, 3, 128], P('gx', 'gy')
- x_core: float32 [128, 3, 128, 128], P('gy', None, 'gx')
All inputs are finite; a program needn't handle non-finite values.
Results may differ from a plain program's by a relative error of at most 0.0003.
Values sent between devices are 32-bit elements; how exact they have to be, the bound alone decides.
No kernel may reach another device: no remote copies, remote signals or barrier semaphores. Data moves between devices by JAX's collectives and lax.ppermute only.
A program may use at most 128 MiB of HBM per device.

v0:
```python
import jax
import jax.numpy as jnp
from jax import lax
from jax.sharding import PartitionSpec as P

POWER = 3


HIGH = lax.Precision.HIGHEST


def orthonormal(mat):
    gram = jnp.dot(mat.T, mat, precision=HIGH, preferred_element_type=jnp.float32)
    lower = jnp.linalg.cholesky(gram)
    return jax.scipy.linalg.solve_triangular(lower, mat.T, lower=True).T


def leading_basis(partial_value, sketch):
    gram = lax.psum(partial_value, ("gx", "gy"))

    def product(mat):
        return jnp.dot(gram, mat, precision=HIGH, preferred_element_type=jnp.float32)

    basis = orthonormal(product(sketch))
    for step in range(POWER - 1):
        basis = orthonormal(product(basis))
    return basis


def shards(motion, time_sketch, x_sketch):
    cx_local, cy_local, comps, steps = motion.shape
    n_gx = lax.axis_size("gx")
    n_gy = lax.axis_size("gy")
    flat = motion.reshape(cx_local * cy_local * comps, steps)
    partial_value = lax.dot_general(
        flat, flat, (((0,), (0,)), ((), ())), precision=HIGH, preferred_element_type=jnp.float32
    )
    partial_value = partial_value / (cx_local * n_gx * cy_local * n_gy * comps)
    time_basis = leading_basis(partial_value, time_sketch)
    ranks = time_basis.shape[1]
    time_core = jnp.dot(
        flat, time_basis, precision=HIGH, preferred_element_type=jnp.float32
    ).reshape(cx_local, cy_local, comps, ranks)
    grouped = lax.all_to_all(time_core, "gx", split_axis=3, concat_axis=0, tiled=True)
    full_x = grouped.shape[0]
    cols = grouped.reshape(full_x, cy_local * comps * (ranks // n_gx))
    x_partial = jnp.dot(cols, cols.T, precision=HIGH, preferred_element_type=jnp.float32) / (
        cy_local * n_gy * comps * ranks
    )
    x_basis = leading_basis(x_partial, x_sketch)
    x_core = lax.dot_general(
        cols, x_basis, (((0,), (0,)), ((), ())), precision=HIGH, preferred_element_type=jnp.float32
    )
    return (time_core, x_core.reshape(cy_local, comps, ranks // n_gx, x_basis.shape[1]))


def solution(mesh):
    in_specs = (P("gx", "gy", None, None), P(), P())
    out_specs = (P("gx", "gy", None, None), P("gy", None, "gx", None))
    return jax.shard_map(shards, mesh=mesh, in_specs=in_specs, out_specs=out_specs, check_vma=False)
```

profile of v0, /device:TPU:0, one launch (start us, length us, event | category | flops | bytes accessed | tf_op | source)
XLA Modules:
  0.0 526.8 jit_solution(11924913601494401581)
XLA Ops:
  7.2 20.9 %fusion = f32[512,512]{1,0:T(8,128)} fusion(f32[96,16,3,512]{3,1,2,0:T(8,128)} %param.8), kind=kOutput, calls=%fused_computation.2 | convolution fusion | flops 14495776768 | bytes 10485760 | tf_op jit(solution)/shard_map/dot_general | solution.py:35
  28.2 14.8 %copy.63 = f32[96,16,3,512]{3,2,1,0:T(4,128)} copy(f32[96,16,3,512]{3,1,2,0:T(8,128)} %param.8) | data formatting | bytes 18874368 | tf_op args[0]
  43.0 15.2 %reshape.27 = f32[4608,512]{1,0:T(8,128)} reshape(f32[96,16,3,512]{3,2,1,0:T(4,128)} %copy.63) | data formatting | bytes 18874368 | tf_op jit(solution)/shard_map/reshape | solution.py:34
  58.2 102.7 %all-reduce.3.cloned.1.call-done = f32[512,512]{1,0:T(8,128)} async-done(((f32[512,512]{1,0:T(8,128)}), f32[512,512]{1,0:T(8,128)}) %all-reduce.3.cloned.1.call-update) | async-done | bytes 1048592 | tf_op jit(solution)/shard_map/psum | solution.py:19
  163.9 11.7 %cholesky.104 = f32[128,128]{1,0:T(8,128)S(1)} custom-call(f32[128,128]{1,0:T(8,128)S(1)} %fusion.29), custom_call_target="Cholesky" | custom-call | tf_op jit(solution)/shard_map/jit(cholesky)/cholesky | solution.py:14
  176.9 9.8 %custom-call.12 = f32[1,128,128]{1,2,0:T(8,128)S(1)} custom-call(f32[1,128,128]{2,1,0:T(8,128)S(1)} %fusion.12), custom_call_target="InvertDiagBlocksLowerTriangular" | custom-call | tf_op jit(solution)/shard_map/jit(_solve_triangular)/triangular_solve | solution.py:15
  188.9 11.9 %cholesky.115 = f32[128,128]{1,0:T(8,128)S(1)} custom-call(f32[128,128]{1,0:T(8,128)S(1)} %fusion.27), custom_call_target="Cholesky" | custom-call | tf_op jit(solution)/shard_map/jit(cholesky)/cholesky | solution.py:14
  202.1 9.8 %custom-call.13 = f32[1,128,128]{1,2,0:T(8,128)S(1)} custom-call(f32[1,128,128]{2,1,0:T(8,128)S(1)} %fusion.13), custom_call_target="InvertDiagBlocksLowerTriangular" | custom-call | tf_op jit(solution)/shard_map/jit(_solve_triangular)/triangular_solve | solution.py:15
  214.0 11.7 %cholesky.126 = f32[128,128]{1,0:T(8,128)S(1)} custom-call(f32[128,128]{1,0:T(8,128)S(1)} %fusion.25), custom_call_target="Cholesky" | custom-call | tf_op jit(solution)/shard_map/jit(cholesky)/cholesky | solution.py:14
  227.1 9.8 %custom-call.14 = f32[1,128,128]{1,2,0:T(8,128)S(1)} custom-call(f32[1,128,128]{2,1,0:T(8,128)S(1)} %fusion.14), custom_call_target="InvertDiagBlocksLowerTriangular" | custom-call | tf_op jit(solution)/shard_map/jit(_solve_triangular)/triangular_solve | solution.py:15
  237.3 12.5 %convolution_bitcast_fusion = f32[4608,128]{0,1:T(8,128)S(1)} fusion(f32[128,512]{1,0:T(8,128)S(1)} %fusion.1, f32[4608,512]{1,0:T(8,128)} %reshape.27), kind=kOutput, calls=%fused_computation | convolution fusion | flops 3623878656 | bytes 12058624 | tf_op jit(solution)/shard_map/dot_general | solution.py:41
  251.8 3.5 reshape.28
  258.4 40.6 %all_to_all.15 = f32[96,16,3,128]{0,1,2,3:T(8,128)S(1)} all-to-all(f32[96,16,3,128]{0,1,2,3:T(8,128)} %copy.65), channel_id=1, replica_groups=mesh['gx'=4,'gy'=8] {'gx'}, dimensions={3} | all-to-all | bytes 4718592 | tf_op jit(solution)/shard_map/all_to_all | solution.py:44
  299.0 3.7 copy.67
  302.7 3.5 reshape.29
  306.3 4.7 convolution_multiply_fusion
  311.0 3.5 copy.71
  314.5 122.8 %all-reduce.5.cloned.1.call-done = f32[384,384]{1,0:T(8,128)} async-done(((f32[384,384]{1,0:T(8,128)}), f32[384,384]{1,0:T(8,128)}) %all-reduce.5.cloned.1.call-update) | async-done | bytes 589840 | tf_op jit(solution)/shard_map/psum | solution.py:19
  440.4 12.5 %cholesky.137 = f32[128,128]{1,0:T(8,128)S(1)} custom-call(f32[128,128]{1,0:T(8,128)} %fusion.23), custom_call_target="Cholesky" | custom-call | tf_op jit(solution)/shard_map/jit(cholesky)/cholesky | solution.py:14
  454.3 9.8 %custom-call.15 = f32[1,128,128]{1,2,0:T(8,128)S(1)} custom-call(f32[1,128,128]{2,1,0:T(8,128)S(1)} %fusion.15), custom_call_target="InvertDiagBlocksLowerTriangular" | custom-call | tf_op jit(solution)/shard_map/jit(_solve_triangular)/triangular_solve | solution.py:15
  467.7 12.5 %cholesky.148 = f32[128,128]{1,0:T(8,128)S(1)} custom-call(f32[128,128]{1,0:T(8,128)} %fusion.21), custom_call_target="Cholesky" | custom-call | tf_op jit(solution)/shard_map/jit(cholesky)/cholesky | solution.py:14
  481.6 9.8 %custom-call.16 = f32[1,128,128]{1,2,0:T(8,128)S(1)} custom-call(f32[1,128,128]{2,1,0:T(8,128)S(1)} %fusion.16), custom_call_target="InvertDiagBlocksLowerTriangular" | custom-call | tf_op jit(solution)/shard_map/jit(_solve_triangular)/triangular_solve | solution.py:15
  493.0 11.9 %cholesky.159 = f32[128,128]{1,0:T(8,128)S(1)} custom-call(f32[128,128]{1,0:T(8,128)S(1)} %fusion.19), custom_call_target="Cholesky" | custom-call | tf_op jit(solution)/shard_map/jit(cholesky)/cholesky | solution.py:14
  506.3 9.8 %custom-call.17 = f32[1,128,128]{1,2,0:T(8,128)S(1)} custom-call(f32[1,128,128]{2,1,0:T(8,128)S(1)} %fusion.17), custom_call_target="InvertDiagBlocksLowerTriangular" | custom-call | tf_op jit(solution)/shard_map/jit(_solve_triangular)/triangular_solve | solution.py:15
  (63 shorter events, 32.3 us)
Async XLA Ops:
  7.2 153.7 %copy-start = (f32[512,128]{1,0:T(8,128)S(1)}, f32[512,128]{1,0:T(8,128)}, u32[]{:S(2)}) copy-start(f32[512,128]{1,0:T(8,128)} %param.9) | copy-start | bytes 786436
  7.2 153.7 %all-reduce.3.cloned.1.call-start = ((), (), s32[]{:S(2)}) async-start(), calls=%async_computation.1 | async-start | bytes 2097152 | tf_op jit(solution)/shard_map/psum | solution.py:19
  28.2 409.1 %all-reduce.5.cloned.1.call-start = ((), (), s32[]{:S(2)}) async-start(), calls=%async_computation.2 | async-start | bytes 1179648 | tf_op jit(solution)/shard_map/psum | solution.py:19
  160.9 26.3 %copy-start.2 = (f32[512,512]{1,0:T(8,128)S(1)}, f32[512,512]{1,0:T(8,128)}, u32[]{:S(2)}) copy-start(f32[512,512]{1,0:T(8,128)} %all-reduce.3.cloned.1.call-done) | copy-start | bytes 3145732
  255.3 3.1 copy-start.1
  437.3 54.5 %copy-start.3 = (f32[384,384]{1,0:T(8,128)S(1)}, f32[384,384]{1,0:T(8,128)}, u32[]{:S(2)}) copy-start(f32[384,384]{1,0:T(8,128)} %all-reduce.5.cloned.1.call-done) | copy-start | bytes 1769476
Sparse Core Ops, SparseCore 0:
  28.3 132.4 all-reduce.2
  311.1 126.1 all-reduce.4
where the time goes:
time: 534 us; the launch traced here: 527 us
  waiting for transfers between devices  226 us (42%)
  other arithmetic  141 us (26%)
  matrix products  55.4 us (10%)
  local copies, waits for them, and re-layouts  49.8 us (9%)
  blocking collectives  40.6 us (8%)
  between operations  14.9 us (3%)
    psum x2, waiting for transfers between devices, leading_basis(): gram = lax.psum(partial_value, ('gx', 'gy'))  225 us
    another operation x18, other arithmetic, orthonormal(): lower = jnp.linalg.cholesky(gram)  76.4 us
    another operation x12, other arithmetic, orthonormal(): return jax.scipy.linalg.solve_triangular(lower, mat.T, lower=True).T  62.8 us
    all_to_all x1, blocking collectives, shards(): lax.all_to_all(time_core, 'gx', split_axis=3, concat_axis=0, tiled=True)  40.6 us
    dot_general x1, matrix products, shards(): lax.dot_general(flat, flat, (((0,), (0,)), ((), ())), precision=HIGH, pre...  20.9 us
    unnamed x10, local copies, waits for them, and re-layouts  18.3 us
    reshape x1, local copies, waits for them, and re-layouts, shards(): flat = motion.reshape(cx_local * cy_local * comps, steps)  15.2 us
    dot_general x1, matrix products, shards(): jnp.dot(flat, time_basis, precision=HIGH, preferred_element_type=jnp.floa...  12.5 us
  transfers between devices with their start and end apart: 2, of which 2 were waited for; matrix products, arithmetic and copies ran while one was open for 6% of the time, Pallas kernels for 0%

commit v1 on v0

v1 whole, which is shorter than its diff:
```python
import jax
import jax.numpy as jnp
from jax import lax
from jax.sharding import PartitionSpec as P

POWER = 3
BLOCK = 128
HIGH = lax.Precision.HIGH
HIGHEST = lax.Precision.HIGHEST


def exchange(value, axis, mask):
    size = lax.axis_size(axis)
    return lax.ppermute(value, axis, [(i, i ^ mask) for i in range(size)])


def bits_of(size):
    bits = []
    mask = 1
    while mask < size:
        bits.append(mask)
        mask *= 2
    return bits


def sum_all(buf):
    steps = [("gx", m) for m in bits_of(lax.axis_size("gx"))]
    steps += [("gy", m) for m in bits_of(lax.axis_size("gy"))]
    halved = []
    for axis, mask in steps:
        rows = buf.shape[0]
        if rows % 16:
            buf = buf + exchange(buf, axis, mask)
            continue
        upper = (lax.axis_index(axis) & mask) != 0
        low, high = buf[: rows // 2], buf[rows // 2 :]
        got = exchange(jnp.where(upper, low, high), axis, mask)
        buf = jnp.where(upper, high, low) + got
        halved.append((axis, mask, upper))
    for axis, mask, upper in reversed(halved):
        got = exchange(buf, axis, mask)
        buf = jnp.where(upper, jnp.concatenate([got, buf]), jnp.concatenate([buf, got]))
    return buf


def sum_gram(partial):
    n = partial.shape[0] // BLOCK
    pairs = [(i, j) for i in range(n) for j in range(i, n)]

    def block(i, j):
        return partial[i * BLOCK : (i + 1) * BLOCK, j * BLOCK : (j + 1) * BLOCK]

    packed = sum_all(jnp.concatenate([block(i, j) for i, j in pairs]))
    at = {pair: packed[k * BLOCK : (k + 1) * BLOCK] for k, pair in enumerate(pairs)}
    return jnp.concatenate(
        [
            jnp.concatenate([at[i, j] if i <= j else at[j, i].T for j in range(n)], axis=1)
            for i in range(n)
        ]
    )


def orthonormal(mat):
    gram = jnp.dot(mat.T, mat, precision=HIGHEST, preferred_element_type=jnp.float32)
    lower = jnp.linalg.cholesky(gram)
    return jax.scipy.linalg.solve_triangular(lower, mat.T, lower=True).T


def leading_basis(partial_value, sketch):
    gram = sum_gram(partial_value)

    def product(mat):
        return jnp.dot(gram, mat, precision=HIGHEST, preferred_element_type=jnp.float32)

    basis = orthonormal(product(sketch))
    for step in range(POWER - 1):
        basis = orthonormal(product(basis))
    return basis


def shards(motion, time_sketch, x_sketch):
    cx_local, cy_local, comps, steps = motion.shape
    n_gx = lax.axis_size("gx")
    n_gy = lax.axis_size("gy")
    flat = motion.transpose(0, 2, 1, 3).reshape(cx_local * comps * cy_local, steps)
    partial_value = lax.dot_general(
        flat, flat, (((0,), (0,)), ((), ())), precision=HIGH, preferred_element_type=jnp.float32
    )
    partial_value = partial_value / (cx_local * n_gx * cy_local * n_gy * comps)
    time_basis = leading_basis(partial_value, time_sketch)
    ranks = time_basis.shape[1]
    share = ranks // n_gx
    core = jnp.dot(flat, time_basis, precision=HIGH, preferred_element_type=jnp.float32)
    time_core = core.reshape(cx_local, comps, cy_local, ranks).transpose(0, 2, 1, 3)

    columns = comps * cy_local * share
    parts = core.reshape(cx_local, comps * cy_local, n_gx, share).transpose(2, 0, 1, 3)
    parts = parts.reshape(n_gx, cx_local, columns)
    mine = lax.axis_index("gx")
    cols = jnp.zeros((n_gx, cx_local, columns), jnp.float32)
    for mask in range(n_gx):
        part = lax.dynamic_index_in_dim(parts, mine ^ mask, 0, keepdims=False)
        if mask:
            part = exchange(part, "gx", mask)
        cols = lax.dynamic_update_index_in_dim(cols, part, mine ^ mask, 0)
    cols = cols.reshape(n_gx * cx_local, columns)

    x_partial = jnp.dot(cols, cols.T, precision=HIGH, preferred_element_type=jnp.float32) / (
        cy_local * n_gy * comps * ranks
    )
    x_basis = leading_basis(x_partial, x_sketch)
    x_core = lax.dot_general(
        cols, x_basis, (((0,), (0,)), ((), ())), precision=HIGH, preferred_element_type=jnp.float32
    )
    x_core = x_core.reshape(comps, cy_local, share, x_basis.shape[1]).transpose(1, 0, 2, 3)
    return (time_core, x_core)


def solution(mesh):
    in_specs = (P("gx", "gy", None, None), P(), P())
    out_specs = (P("gx", "gy", None, None), P("gy", None, "gx", None))
    return jax.shard_map(shards, mesh=mesh, in_specs=in_specs, out_specs=out_specs, check_vma=False)
```

time: 534 us -> 311 us (0.58)
  waiting for transfers between devices: 226 us -> 68.2 us
  blocking collectives: 40.6 us -> 0 us
  starting transfers between devices: 0.08 us -> 36 us
  local copies, waits for them, and re-layouts: 49.8 us -> 28.1 us
  matrix products: 55.4 us -> 34.8 us
  between operations: 14.9 us -> 1.95 us
    psum x2 -> x0, waiting for transfers between devices: 225 us -> none  [leading_basis(): gram = lax.psum(partial_value, ('gx', 'gy'))]
    ppermute x0 -> x23, waiting for transfers between devices: none -> 68.2 us  [exchange(): return lax.ppermute(value, axis, [(i, i ^ mask) for i in range(size)])]
    all_to_all x1 -> x0, blocking collectives: 40.6 us -> none  [shards(): lax.all_to_all(time_core, 'gx', split_axis=3, concat_axis=0, tiled=True)]
    ppermute x0 -> x23, starting transfers between devices: none -> 36 us  [exchange(): return lax.ppermute(value, axis, [(i, i ^ mask) for i in range(size)])]
    reshape x4 -> x1, local copies, waits for them, and re-layouts: 25.3 us -> 4.45 us  [shards(): core.reshape(cx_local, comps * cy_local, n_gx, share).transpose(2, 0, 1, 3)]
    unnamed x10 -> x25, local copies, waits for them, and re-layouts: 18.3 us -> 1.83 us
    dot_general x1, matrix products: 20.9 us -> 11.9 us  [shards(): lax.dot_general(flat, flat, (((0,), (0,)), ((), ())), precision=HIGH, pre...]
    dynamic_slice x0 -> x5, local copies, waits for them, and re-layouts: none -> 7.58 us  [shards(): part = lax.dynamic_index_in_dim(parts, mine ^ mask, 0, keepdims=False)]
  transfers between devices with their start and end apart: 2 -> 23, of which waited for: 2 -> 21; matrix products, arithmetic and copies ran while one was open for 6% -> 4% of each run, Pallas kernels for 0% -> 0%
where the time goes in v1:
time: 311 us; the launch traced here: 307 us
  other arithmetic  138 us (44%)
  waiting for transfers between devices  68.2 us (22%)
  starting transfers between devices  36 us (12%)
  matrix products  34.8 us (11%)
  local copies, waits for them, and re-layouts  28.1 us (9%)
    another operation x18, other arithmetic, orthonormal(): lower = jnp.linalg.cholesky(gram)  74.9 us
    ppermute x23, waiting for transfers between devices, exchange(): return lax.ppermute(value, axis, [(i, i ^ mask) for i in range(size)])  68.2 us
    another operation x12, other arithmetic, orthonormal(): return jax.scipy.linalg.solve_triangular(lower, mat.T, lower=True).T  62.8 us
    ppermute x23, starting transfers between devices, exchange(): return lax.ppermute(value, axis, [(i, i ^ mask) for i in range(size)])  36 us
    dot_general x1, matrix products, shards(): lax.dot_general(flat, flat, (((0,), (0,)), ((), ())), precision=HIGH, pre...  11.9 us
    dot_general x1, matrix products, shards(): jnp.dot(flat, time_basis, precision=HIGH, preferred_element_type=jnp.floa...  8.44 us
    dynamic_slice x5, local copies, waits for them, and re-layouts, shards(): part = lax.dynamic_index_in_dim(parts, mine ^ mask, 0, keepdims=False)  7.58 us
  transfers between devices with their start and end apart: 23, of which 21 were waited for; matrix products, arithmetic and copies ran while one was open for 4% of the time, Pallas kernels for 0%

profile of v1, /device:TPU:0, one launch (start us, length us, event | category | flops | bytes accessed | tf_op | source)
XLA Modules:
  0.0 307.4 jit_solution(15474663000014081293)
XLA Ops:
  0.6 11.9 %fusion.5 = f32[512,512]{1,0:T(8,128)S(1)} fusion(f32[96,16,3,512]{3,1,2,0:T(8,128)} %param.8), kind=kOutput, calls=%fused_computation.4 | convolution fusion | flops 7248019456 | bytes 10485760 | tf_op jit(solution)/shard_map/dot_general | solution.py:86
  17.5 4.5 %collective-permute-done.1 = f32[320,128]{1,0:T(8,128)S(1)} collective-permute-done((f32[320,128]{1,0:T(8,128)S(1)}, f32[320,128]{1,0:T(8,128)S(1)}, u32[]{:S(2)}, u32[]{:S(2)}) %collective-permute-start.1) | collective-permute-done | bytes 163872 | tf_op jit(solution)/shard_map/ppermute | solution.py:14
  30.7 3.1 %collective-permute-start.4 = (f32[40,128]{1,0:T(8,128)S(1)}, f32[40,128]{1,0:T(8,128)S(1)}, u32[]{:S(2)}, u32[]{:S(2)}) collective-permute-start(f32[40,128]{1,0:T(8,128)S(1)} %slice_select_fusion.6), channel_id=1, source_target_pairs={{0,4},{1,5},{2,6},{3,7},{4,0},{5,1},{6,2},{7,3},{8,12},{9,13},{10,... | collective-permute-start | bytes 61448 | tf_op jit(solution)/shard_map/ppermute | solution.py:14
  50.5 3.8 %collective-permute-done.8 = f32[320,128]{1,0:T(8,128)S(1)} collective-permute-done((f32[320,128]{1,0:T(8,128)S(1)}, f32[320,128]{1,0:T(8,128)S(1)}, u32[]{:S(2)}, u32[]{:S(2)}) %collective-permute-start.8) | collective-permute-done | bytes 163872 | tf_op jit(solution)/shard_map/ppermute | solution.py:14
  58.7 11.7 %cholesky.104 = f32[128,128]{1,0:T(8,128)S(1)} custom-call(f32[128,128]{1,0:T(8,128)S(1)} %fusion.38), custom_call_target="Cholesky" | custom-call | tf_op jit(solution)/shard_map/jit(cholesky)/cholesky | solution.py:65
  71.8 9.8 %custom-call.12 = f32[1,128,128]{1,2,0:T(8,128)S(1)} custom-call(f32[1,128,128]{2,1,0:T(8,128)S(1)} %fusion.21), custom_call_target="InvertDiagBlocksLowerTriangular" | custom-call | tf_op jit(solution)/shard_map/jit(_solve_triangular)/triangular_solve | solution.py:66
  83.7 12.1 %cholesky.115 = f32[128,128]{1,0:T(8,128)S(1)} custom-call(f32[128,128]{1,0:T(8,128)S(1)} %fusion.36), custom_call_target="Cholesky" | custom-call | tf_op jit(solution)/shard_map/jit(cholesky)/cholesky | solution.py:65
  97.2 9.8 %custom-call.13 = f32[1,128,128]{1,2,0:T(8,128)S(1)} custom-call(f32[1,128,128]{2,1,0:T(8,128)S(1)} %fusion.22), custom_call_target="InvertDiagBlocksLowerTriangular" | custom-call | tf_op jit(solution)/shard_map/jit(_solve_triangular)/triangular_solve | solution.py:66
  109.1 11.7 %cholesky.126 = f32[128,128]{1,0:T(8,128)S(1)} custom-call(f32[128,128]{1,0:T(8,128)S(1)} %fusion.34), custom_call_target="Cholesky" | custom-call | tf_op jit(solution)/shard_map/jit(cholesky)/cholesky | solution.py:65
  122.1 9.9 %custom-call.14 = f32[1,128,128]{1,2,0:T(8,128)S(1)} custom-call(f32[1,128,128]{2,1,0:T(8,128)S(1)} %fusion.23), custom_call_target="InvertDiagBlocksLowerTriangular" | custom-call | tf_op jit(solution)/shard_map/jit(_solve_triangular)/triangular_solve | solution.py:66
  132.5 8.4 %convolution_bitcast_fusion = f32[4608,128]{0,1:T(8,128)S(1)} fusion(f32[128,512]{1,0:T(8,128)S(1)} %fusion.8, f32[4608,512]{1,0:T(8,128)} %bitcast.160), kind=kOutput, calls=%fused_computation.2 | convolution fusion | flops 1811939328 | bytes 12058624 | tf_op jit(solution)/shard_map/dot_general | solution.py:93
  141.0 4.4 %reshape.34 = f32[96,48,4,32]{1,0,3,2:T(8,128)} reshape(f32[4608,128]{0,1:T(8,128)S(1)} %convolution_bitcast_fusion) | data formatting | bytes 4718592 | tf_op jit(solution)/shard_map/reshape | solution.py:97
  145.4 5.1 %copy.63 = f32[4,96,48,32]{1,3,2,0:T(8,128)S(1)} copy(f32[4,96,48,32]{2,1,3,0:T(8,128)} %bitcast.158) | data formatting | bytes 4718592 | tf_op jit(solution)/shard_map/transpose | solution.py:97
  161.5 12.2 %collective-permute-done.11 = f32[96,1536]{1,0:T(8,128)} collective-permute-done((f32[96,1536]{1,0:T(8,128)}, f32[96,1536]{1,0:T(8,128)}, u32[]{:S(2)}, u32[]{:S(2)}) %collective-permute-start.11) | collective-permute-done | bytes 589856 | tf_op jit(solution)/shard_map/ppermute | solution.py:14
  174.8 10.3 %collective-permute-done.12 = f32[96,1536]{1,0:T(8,128)S(1)} collective-permute-done((f32[96,1536]{1,0:T(8,128)}, f32[96,1536]{1,0:T(8,128)S(1)}, u32[]{:S(2)}, u32[]{:S(2)}) %collective-permute-start.12) | collective-permute-done | bytes 589856 | tf_op jit(solution)/shard_map/ppermute | solution.py:14
  190.5 3.5 %collective-permute-done.14 = f32[192,128]{1,0:T(8,128)S(1)} collective-permute-done((f32[192,128]{1,0:T(8,128)S(1)}, f32[192,128]{1,0:T(8,128)S(1)}, u32[]{:S(2)}, u32[]{:S(2)}) %collective-permute-start.14) | collective-permute-done | bytes 98336 | tf_op jit(solution)/shard_map/ppermute | solution.py:14
  202.1 3.1 %collective-permute-start.17 = (f32[24,128]{1,0:T(8,128)S(1)}, f32[24,128]{1,0:T(8,128)S(1)}, u32[]{:S(2)}, u32[]{:S(2)}) collective-permute-start(f32[24,128]{1,0:T(8,128)S(1)} %slice_select_fusion.7), channel_id=1, source_target_pairs={{0,4},{1,5},{2,6},{3,7},{4,0},{5,1},{6,2},{7,3},{8,12},{9,13},{10,... | collective-permute-start | bytes 36872 | tf_op jit(solution)/shard_map/ppermute | solution.py:14
  221.1 3.1 %collective-permute-done.21 = f32[192,128]{1,0:T(8,128)S(1)} collective-permute-done((f32[192,128]{1,0:T(8,128)S(1)}, f32[192,128]{1,0:T(8,128)S(1)}, u32[]{:S(2)}, u32[]{:S(2)}) %collective-permute-start.21) | collective-permute-done | bytes 98336 | tf_op jit(solution)/shard_map/ppermute | solution.py:14
  231.7 11.7 %cholesky.137 = f32[128,128]{1,0:T(8,128)S(1)} custom-call(f32[128,128]{1,0:T(8,128)S(1)} %fusion.32), custom_call_target="Cholesky" | custom-call | tf_op jit(solution)/shard_map/jit(cholesky)/cholesky | solution.py:65
  244.6 9.8 %custom-call.15 = f32[1,128,128]{1,2,0:T(8,128)S(1)} custom-call(f32[1,128,128]{2,1,0:T(8,128)S(1)} %fusion.24), custom_call_target="InvertDiagBlocksLowerTriangular" | custom-call | tf_op jit(solution)/shard_map/jit(_solve_triangular)/triangular_solve | solution.py:66
  256.1 11.9 %cholesky.148 = f32[128,128]{1,0:T(8,128)S(1)} custom-call(f32[128,128]{1,0:T(8,128)S(1)} %fusion.30), custom_call_target="Cholesky" | custom-call | tf_op jit(solution)/shard_map/jit(cholesky)/cholesky | solution.py:65
  269.3 9.8 %custom-call.16 = f32[1,128,128]{1,2,0:T(8,128)S(1)} custom-call(f32[1,128,128]{2,1,0:T(8,128)S(1)} %fusion.25), custom_call_target="InvertDiagBlocksLowerTriangular" | custom-call | tf_op jit(solution)/shard_map/jit(_solve_triangular)/triangular_solve | solution.py:66
  281.6 11.7 %cholesky.159 = f32[128,128]{1,0:T(8,128)S(1)} custom-call(f32[128,128]{1,0:T(8,128)S(1)} %fusion.28), custom_call_target="Cholesky" | custom-call | tf_op jit(solution)/shard_map/jit(cholesky)/cholesky | solution.py:65
  294.7 9.8 %custom-call.17 = f32[1,128,128]{1,2,0:T(8,128)S(1)} custom-call(f32[1,128,128]{2,1,0:T(8,128)S(1)} %fusion.26), custom_call_target="InvertDiagBlocksLowerTriangular" | custom-call | tf_op jit(solution)/shard_map/jit(_solve_triangular)/triangular_solve | solution.py:66
  (170 shorter events, 102.0 us)
Async XLA Ops:
  0.6 56.4 %copy-start = (f32[512,128]{1,0:T(8,128)S(1)}, f32[512,128]{1,0:T(8,128)}, u32[]{:S(2)}) copy-start(f32[512,128]{1,0:T(8,128)} %param.9) | copy-start | bytes 786436
  12.7 1.8 collective-permute-start
  14.6 7.5 %collective-permute-start.1 = (f32[320,128]{1,0:T(8,128)S(1)}, f32[320,128]{1,0:T(8,128)S(1)}, u32[]{:S(2)}, u32[]{:S(2)}) collective-permute-start(f32[320,128]{1,0:T(8,128)S(1)} %slice_select_fusion), channel_id=1, source_target_pairs={{0,16},{8,24},{16,0},{24,8},{1,17},{9,25},{17,1},{25,9},{2,18},{10... | collective-permute-start | bytes 491528 | tf_op jit(solution)/shard_map/ppermute | solution.py:14
  22.1 4.5 %collective-permute-start.2 = (f32[160,128]{1,0:T(8,128)S(1)}, f32[160,128]{1,0:T(8,128)S(1)}, u32[]{:S(2)}, u32[]{:S(2)}) collective-permute-start(f32[160,128]{1,0:T(8,128)S(1)} %slice_select_fusion.2), channel_id=1, source_target_pairs={{0,1},{1,0},{2,3},{3,2},{4,5},{5,4},{6,7},{7,6},{8,9},{9,8},{10,11... | collective-permute-start | bytes 245768 | tf_op jit(solution)/shard_map/ppermute | solution.py:14
  26.6 4.1 %collective-permute-start.3 = (f32[80,128]{1,0:T(8,128)S(1)}, f32[80,128]{1,0:T(8,128)S(1)}, u32[]{:S(2)}, u32[]{:S(2)}) collective-permute-start(f32[80,128]{1,0:T(8,128)S(1)} %slice_select_fusion.4), channel_id=1, source_target_pairs={{0,2},{1,3},{2,0},{3,1},{4,6},{5,7},{6,4},{7,5},{8,10},{9,11},{10,... | collective-permute-start | bytes 122888 | tf_op jit(solution)/shard_map/ppermute | solution.py:14
  30.7 4.9 %collective-permute-start.4 = (f32[40,128]{1,0:T(8,128)S(1)}, f32[40,128]{1,0:T(8,128)S(1)}, u32[]{:S(2)}, u32[]{:S(2)}) collective-permute-start(f32[40,128]{1,0:T(8,128)S(1)} %slice_select_fusion.6), channel_id=1, source_target_pairs={{0,4},{1,5},{2,6},{3,7},{4,0},{5,1},{6,2},{7,3},{8,12},{9,13},{10,... | collective-permute-start | bytes 61448 | tf_op jit(solution)/shard_map/ppermute | solution.py:14
  35.6 4.8 %collective-permute-start.5 = (f32[40,128]{1,0:T(8,128)S(1)}, f32[40,128]{1,0:T(8,128)S(1)}, u32[]{:S(2)}, u32[]{:S(2)}) collective-permute-start(f32[40,128]{1,0:T(8,128)S(1)} %select_add_fusion.8), channel_id=1, source_target_pairs={{0,4},{1,5},{2,6},{3,7},{4,0},{5,1},{6,2},{7,3},{8,12},{9,13},{10,... | collective-permute-start | bytes 61448 | tf_op jit(solution)/shard_map/ppermute | solution.py:14
  40.4 4.0 %collective-permute-start.6 = (f32[80,128]{1,0:T(8,128)S(1)}, f32[80,128]{1,0:T(8,128)S(1)}, u32[]{:S(2)}, u32[]{:S(2)}) collective-permute-start(f32[80,128]{1,0:T(8,128)S(1)} %maximum_select_fusion.8), channel_id=1, source_target_pairs={{0,2},{1,3},{2,0},{3,1},{4,6},{5,7},{6,4},{7,5},{8,10},{9,11},{10,... | collective-permute-start | bytes 122888 | tf_op jit(solution)/shard_map/ppermute | solution.py:14
  44.4 4.5 %collective-permute-start.7 = (f32[160,128]{1,0:T(8,128)S(1)}, f32[160,128]{1,0:T(8,128)S(1)}, u32[]{:S(2)}, u32[]{:S(2)}) collective-permute-start(f32[160,128]{1,0:T(8,128)S(1)} %maximum_select_fusion.6), channel_id=1, source_target_pairs={{0,1},{1,0},{2,3},{3,2},{4,5},{5,4},{6,7},{7,6},{8,9},{9,8},{10,11... | collective-permute-start | bytes 245768 | tf_op jit(solution)/shard_map/ppermute | solution.py:14
  48.9 5.4 %collective-permute-start.8 = (f32[320,128]{1,0:T(8,128)S(1)}, f32[320,128]{1,0:T(8,128)S(1)}, u32[]{:S(2)}, u32[]{:S(2)}) collective-permute-start(f32[320,128]{1,0:T(8,128)S(1)} %maximum_select_fusion.4), channel_id=1, source_target_pairs={{0,16},{8,24},{16,0},{24,8},{1,17},{9,25},{17,1},{25,9},{2,18},{10... | collective-permute-start | bytes 491528 | tf_op jit(solution)/shard_map/ppermute | solution.py:14
  54.3 1.7 collective-permute-start.9
  154.6 5.8 %collective-permute-start.10 = (f32[96,1536]{1,0:T(8,128)}, f32[96,1536]{1,0:T(8,128)}, u32[]{:S(2)}, u32[]{:S(2)}) collective-permute-start(f32[96,1536]{1,0:T(8,128)} %bitcast.27), channel_id=1, source_target_pairs={{0,8},{8,0},{16,24},{24,16},{1,9},{9,1},{17,25},{25,17},{2,10},{10... | collective-permute-start | bytes 1769480 | tf_op jit(solution)/shard_map/ppermute | solution.py:14
  157.2 16.5 %collective-permute-start.11 = (f32[96,1536]{1,0:T(8,128)}, f32[96,1536]{1,0:T(8,128)}, u32[]{:S(2)}, u32[]{:S(2)}) collective-permute-start(f32[96,1536]{1,0:T(8,128)} %bitcast.29), channel_id=1, source_target_pairs={{0,16},{8,24},{16,0},{24,8},{1,17},{9,25},{17,1},{25,9},{2,18},{10... | collective-permute-start | bytes 1769480 | tf_op jit(solution)/shard_map/ppermute | solution.py:14
  159.9 25.3 %collective-permute-start.12 = (f32[96,1536]{1,0:T(8,128)}, f32[96,1536]{1,0:T(8,128)S(1)}, u32[]{:S(2)}, u32[]{:S(2)}) collective-permute-start(f32[96,1536]{1,0:T(8,128)} %bitcast.31), channel_id=1, source_target_pairs={{0,24},{8,16},{16,8},{24,0},{1,25},{9,17},{17,9},{25,1},{2,26},{10... | collective-permute-start | bytes 1769480 | tf_op jit(solution)/shard_map/ppermute | solution.py:14
  187.3 1.5 collective-permute-start.13
  188.8 5.1 %collective-permute-start.14 = (f32[192,128]{1,0:T(8,128)S(1)}, f32[192,128]{1,0:T(8,128)S(1)}, u32[]{:S(2)}, u32[]{:S(2)}) collective-permute-start(f32[192,128]{1,0:T(8,128)S(1)} %slice_select_fusion.1), channel_id=1, source_target_pairs={{0,16},{8,24},{16,0},{24,8},{1,17},{9,25},{17,1},{25,9},{2,18},{10... | collective-permute-start | bytes 294920 | tf_op jit(solution)/shard_map/ppermute | solution.py:14
  194.0 4.2 %collective-permute-start.15 = (f32[96,128]{1,0:T(8,128)S(1)}, f32[96,128]{1,0:T(8,128)S(1)}, u32[]{:S(2)}, u32[]{:S(2)}) collective-permute-start(f32[96,128]{1,0:T(8,128)S(1)} %slice_select_fusion.3), channel_id=1, source_target_pairs={{0,1},{1,0},{2,3},{3,2},{4,5},{5,4},{6,7},{7,6},{8,9},{9,8},{10,11... | collective-permute-start | bytes 147464 | tf_op jit(solution)/shard_map/ppermute | solution.py:14
  198.2 3.9 %collective-permute-start.16 = (f32[48,128]{1,0:T(8,128)S(1)}, f32[48,128]{1,0:T(8,128)S(1)}, u32[]{:S(2)}, u32[]{:S(2)}) collective-permute-start(f32[48,128]{1,0:T(8,128)S(1)} %slice_select_fusion.5), channel_id=1, source_target_pairs={{0,2},{1,3},{2,0},{3,1},{4,6},{5,7},{6,4},{7,5},{8,10},{9,11},{10,... | collective-permute-start | bytes 73736 | tf_op jit(solution)/shard_map/ppermute | solution.py:14
  202.1 4.8 %collective-permute-start.17 = (f32[24,128]{1,0:T(8,128)S(1)}, f32[24,128]{1,0:T(8,128)S(1)}, u32[]{:S(2)}, u32[]{:S(2)}) collective-permute-start(f32[24,128]{1,0:T(8,128)S(1)} %slice_select_fusion.7), channel_id=1, source_target_pairs={{0,4},{1,5},{2,6},{3,7},{4,0},{5,1},{6,2},{7,3},{8,12},{9,13},{10,... | collective-permute-start | bytes 36872 | tf_op jit(solution)/shard_map/ppermute | solution.py:14
  207.0 4.6 %collective-permute-start.18 = (f32[24,128]{1,0:T(8,128)S(1)}, f32[24,128]{1,0:T(8,128)S(1)}, u32[]{:S(2)}, u32[]{:S(2)}) collective-permute-start(f32[24,128]{1,0:T(8,128)S(1)} %select_add_fusion.9), channel_id=1, source_target_pairs={{0,4},{1,5},{2,6},{3,7},{4,0},{5,1},{6,2},{7,3},{8,12},{9,13},{10,... | collective-permute-start | bytes 36872 | tf_op jit(solution)/shard_map/ppermute | solution.py:14
  211.6 3.8 %collective-permute-start.19 = (f32[48,128]{1,0:T(8,128)S(1)}, f32[48,128]{1,0:T(8,128)S(1)}, u32[]{:S(2)}, u32[]{:S(2)}) collective-permute-start(f32[48,128]{1,0:T(8,128)S(1)} %maximum_select_fusion.9), channel_id=1, source_target_pairs={{0,2},{1,3},{2,0},{3,1},{4,6},{5,7},{6,4},{7,5},{8,10},{9,11},{10,... | collective-permute-start | bytes 73736 | tf_op jit(solution)/shard_map/ppermute | solution.py:14
  215.4 4.1 %collective-permute-start.20 = (f32[96,128]{1,0:T(8,128)S(1)}, f32[96,128]{1,0:T(8,128)S(1)}, u32[]{:S(2)}, u32[]{:S(2)}) collective-permute-start(f32[96,128]{1,0:T(8,128)S(1)} %maximum_select_fusion.7), channel_id=1, source_target_pairs={{0,1},{1,0},{2,3},{3,2},{4,5},{5,4},{6,7},{7,6},{8,9},{9,8},{10,11... | collective-permute-start | bytes 147464 | tf_op jit(solution)/shard_map/ppermute | solution.py:14
  219.5 4.7 %collective-permute-start.21 = (f32[192,128]{1,0:T(8,128)S(1)}, f32[192,128]{1,0:T(8,128)S(1)}, u32[]{:S(2)}, u32[]{:S(2)}) collective-permute-start(f32[192,128]{1,0:T(8,128)S(1)} %maximum_select_fusion.5), channel_id=1, source_target_pairs={{0,16},{8,24},{16,0},{24,8},{1,17},{9,25},{17,1},{25,9},{2,18},{10... | collective-permute-start | bytes 294920 | tf_op jit(solution)/shard_map/ppermute | solution.py:14
  224.2 5.3 %collective-permute-start.22 = (f32[384,128]{1,0:T(8,128)S(1)}, f32[384,128]{1,0:T(8,128)S(1)}, u32[]{:S(2)}, u32[]{:S(2)}) collective-permute-start(f32[384,128]{1,0:T(8,128)S(1)} %maximum_select_fusion.3), channel_id=1, source_target_pairs={{0,8},{8,0},{16,24},{24,16},{1,9},{9,1},{17,25},{25,17},{2,10},{10... | collective-permute-start | bytes 589832 | tf_op jit(solution)/shard_map/ppermute | solution.py:14
  (6 other events, 90.4 us)

commit v2 on v1

--- a/solution.py
+++ b/solution.py
@@ -1,12 +1,102 @@
 import jax
 import jax.numpy as jnp
 from jax import lax
+from jax.experimental import pallas as pl
+from jax.experimental.pallas import tpu as pltpu
 from jax.sharding import PartitionSpec as P
 
+HIGH = lax.Precision.HIGH
+BLOCK = 128
+PANEL = 16
 POWER = 3
-BLOCK = 128
-HIGH = lax.Precision.HIGH
 HIGHEST = lax.Precision.HIGHEST
+
+
+def dot(a, b, ca, cb):
+    return lax.dot_general(
+        a, b, (((ca,), (cb,)), ((), ())), precision=HIGHEST, preferred_element_type=jnp.float32
+    )
+
+
+def factor_panel(work, splat, rows, start):
+    ranks = work.shape[0]
+    here = pl.ds(start, PANEL)
+    for i in range(PANEL):
+        splat[i] = jnp.broadcast_to(work[here, start + i : start + i + 1], (PANEL, ranks))
+    entry = {(k, i): splat[i, k : k + 1, :] for i in range(PANEL) for k in range(i, PANEL)}
+    done = []
+    for i in range(PANEL):
+        scale = lax.rsqrt(entry[i, i])
+        low = {k: entry[k, i] * scale for k in range(i + 1, PANEL)}
+        for k in range(i + 1, PANEL):
+            for j in range(i + 1, k + 1):
+                entry[k, j] = entry[k, j] - low[k] * low[j]
+        for k in range(i + 1, PANEL):
+            entry[k, i] = low[k]
+        halves = []
+        for half in range(2):
+            row = work[start + i : start + i + 1, half * ranks : (half + 1) * ranks]
+            for k in range(i):
+                row = row - entry[i, k] * done[k][half]
+            row = row * scale
+            rows[start + i : start + i + 1, half * ranks : (half + 1) * ranks] = row
+            halves.append(row)
+        done.append(halves)
+
+
+def basis_kernel(packed_ref, sketch_ref, out_ref, gram, prod, work, rows, splat):
+    size = sketch_ref.shape[0]
+    ranks = sketch_ref.shape[1]
+    n = size // BLOCK
+    at = 0
+    for i in range(n):
+        for j in range(i, n):
+            block = packed_ref[at * BLOCK : (at + 1) * BLOCK, :]
+            gram[i * BLOCK : (i + 1) * BLOCK, j * BLOCK : (j + 1) * BLOCK] = block
+            if i != j:
+                gram[j * BLOCK : (j + 1) * BLOCK, i * BLOCK : (i + 1) * BLOCK] = block.T
+            at += 1
+    prod[...] = dot(sketch_ref[...], gram[...], 0, 0)
+
+    def orthonormal(step, carry):
+        @pl.when(step > 0)
+        def _():
+            prod[...] = dot(out_ref[...], gram[...], 1, 0)
+
+        value = prod[...]
+        work[:, :ranks] = dot(value, value, 1, 1)
+        row = lax.broadcasted_iota(jnp.int32, (ranks, ranks), 0)
+        col = lax.broadcasted_iota(jnp.int32, (ranks, ranks), 1)
+        work[:, ranks:] = jnp.where(row == col, 1.0, 0.0)
+        for start in range(0, ranks, PANEL):
+            factor_panel(work, splat, rows, start)
+            if start + PANEL < ranks:
+                panel = rows[start : start + PANEL, :]
+                rest = start + PANEL
+                work[rest:, :] = work[rest:, :] - dot(panel[:, rest:ranks], panel, 0, 0)
+        out_ref[...] = dot(rows[:, ranks:], prod[...], 1, 0)
+        return carry
+
+    lax.fori_loop(0, POWER, orthonormal, 0)
+
+
+def leading_basis(packed, sketch):
+    size, ranks = sketch.shape
+    return pl.pallas_call(
+        basis_kernel,
+        out_shape=jax.ShapeDtypeStruct((ranks, size), jnp.float32),
+        in_specs=[pl.BlockSpec(memory_space=pltpu.VMEM)] * 2,
+        out_specs=pl.BlockSpec(memory_space=pltpu.VMEM),
+        scratch_shapes=[
+            pltpu.VMEM((size, size), jnp.float32),
+            pltpu.VMEM((ranks, size), jnp.float32),
+            pltpu.VMEM((ranks, 2 * ranks), jnp.float32),
+            pltpu.VMEM((ranks, 2 * ranks), jnp.float32),
+            pltpu.VMEM((PANEL, PANEL, ranks), jnp.float32),
+        ],
+        compiler_params=pltpu.CompilerParams(vmem_limit_bytes=32 * 2**20),
+        name="leading_basis",
+    )(packed, sketch)
 
 
 def exchange(value, axis, mask):
@@ -29,7 +119,7 @@
     halved = []
     for axis, mask in steps:
         rows = buf.shape[0]
-        if rows % 16:
+        if rows % 16 or rows <= 160:
             buf = buf + exchange(buf, axis, mask)
             continue
         upper = (lax.axis_index(axis) & mask) != 0
@@ -50,32 +140,7 @@
     def block(i, j):
         return partial[i * BLOCK : (i + 1) * BLOCK, j * BLOCK : (j + 1) * BLOCK]
 
-    packed = sum_all(jnp.concatenate([block(i, j) for i, j in pairs]))
-    at = {pair: packed[k * BLOCK : (k + 1) * BLOCK] for k, pair in enumerate(pairs)}
-    return jnp.concatenate(
-        [
-            jnp.concatenate([at[i, j] if i <= j else at[j, i].T for j in range(n)], axis=1)
-            for i in range(n)
-        ]
-    )
-
-
-def orthonormal(mat):
-    gram = jnp.dot(mat.T, mat, precision=HIGHEST, preferred_element_type=jnp.float32)
-    lower = jnp.linalg.cholesky(gram)
-    return jax.scipy.linalg.solve_triangular(lower, mat.T, lower=True).T
-
-
-def leading_basis(partial_value, sketch):
-    gram = sum_gram(partial_value)
-
-    def product(mat):
-        return jnp.dot(gram, mat, precision=HIGHEST, preferred_element_type=jnp.float32)
-
-    basis = orthonormal(product(sketch))
-    for step in range(POWER - 1):
-        basis = orthonormal(product(basis))
-    return basis
+    return sum_all(jnp.concatenate([block(i, j) for i, j in pairs]))
 
 
 def shards(motion, time_sketch, x_sketch):
@@ -87,10 +152,10 @@
         flat, flat, (((0,), (0,)), ((), ())), precision=HIGH, preferred_element_type=jnp.float32
     )
     partial_value = partial_value / (cx_local * n_gx * cy_local * n_gy * comps)
-    time_basis = leading_basis(partial_value, time_sketch)
-    ranks = time_basis.shape[1]
+    time_basis = leading_basis(sum_gram(partial_value), time_sketch)
+    ranks = time_basis.shape[0]
     share = ranks // n_gx
-    core = jnp.dot(flat, time_basis, precision=HIGH, preferred_element_type=jnp.float32)
+    core = jnp.dot(flat, time_basis.T, precision=HIGH, preferred_element_type=jnp.float32)
     time_core = core.reshape(cx_local, comps, cy_local, ranks).transpose(0, 2, 1, 3)
 
     columns = comps * cy_local * share
@@ -108,11 +173,11 @@
     x_partial = jnp.dot(cols, cols.T, precision=HIGH, preferred_element_type=jnp.float32) / (
         cy_local * n_gy * comps * ranks
     )
-    x_basis = leading_basis(x_partial, x_sketch)
+    x_basis = leading_basis(sum_gram(x_partial), x_sketch)
     x_core = lax.dot_general(
-        cols, x_basis, (((0,), (0,)), ((), ())), precision=HIGH, preferred_element_type=jnp.float32
+        cols, x_basis, (((0,), (1,)), ((), ())), precision=HIGH, preferred_element_type=jnp.float32
     )
-    x_core = x_core.reshape(comps, cy_local, share, x_basis.shape[1]).transpose(1, 0, 2, 3)
+    x_core = x_core.reshape(comps, cy_local, share, x_basis.shape[0]).transpose(1, 0, 2, 3)
     return (time_core, x_core)
 
 

time: 311 us -> 183 us (0.59); the launches traced: 307 us -> 183 us
  other arithmetic: 138 us -> 0.43 us
  Pallas kernels: 0 us -> 41.5 us
  matrix products: 34.8 us -> 24.9 us
  starting transfers between devices: 36 us -> 27 us
  waiting for transfers between devices: 68.2 us -> 63.1 us
  local copies, waits for them, and re-layouts: 28.1 us -> 24.9 us
    another operation x30 -> x0, other arithmetic: 138 us -> none  [the longest x18 74.9 us: orthonormal(): lower = jnp.linalg.cholesky(gram)]
    pallas_call x0 -> x2, Pallas kernels: none -> 41.5 us  [leading_basis(): pl.pallas_call(basis_kernel, out_shape=jax.ShapeDtypeStruct((ranks, size)...]
    ppermute x23 -> x19, starting transfers between devices: 36 us -> 27 us  [exchange(): return lax.ppermute(value, axis, [(i, i ^ mask) for i in range(size)])]
    dot_general x14 -> x2, matrix products: 18.5 us -> 11.2 us  [the longest x1 8.43 us: shards(): jnp.dot(flat, time_basis.T, precision=HIGH, preferred_element_type=jnp.fl...]
    ppermute x23 -> x19, waiting for transfers between devices: 68.2 us -> 63.1 us  [exchange(): return lax.ppermute(value, axis, [(i, i ^ mask) for i in range(size)])]
  transfers between devices with their start and end apart: 23 -> 19, of which waited for: 21 -> 17; matrix products, arithmetic and copies ran while one was open for 4% -> 5% of each run, Pallas kernels for 0% -> 0%
where the time goes in v2:
time: 183 us
  waiting for transfers between devices  63.1 us (34%)
  Pallas kernels  41.5 us (23%)
  starting transfers between devices  27 us (15%)
  matrix products  24.9 us (14%)
  local copies, waits for them, and re-layouts  24.9 us (14%)
    ppermute x19, waiting for transfers between devices, exchange(): return lax.ppermute(value, axis, [(i, i ^ mask) for i in range(size)])  63.1 us
    pallas_call x2, Pallas kernels, leading_basis(): pl.pallas_call(basis_kernel, out_shape=jax.ShapeDtypeStruct((ranks, size)...  41.5 us
    ppermute x19, starting transfers between devices, exchange(): return lax.ppermute(value, axis, [(i, i ^ mask) for i in range(size)])  27 us
    dot_general x1, matrix products, shards(): lax.dot_general(flat, flat, (((0,), (0,)), ((), ())), precision=HIGH, pre...  11.7 us
    dot_general x1, matrix products, shards(): jnp.dot(flat, time_basis.T, precision=HIGH, preferred_element_type=jnp.fl...  8.43 us
    dynamic_slice x5, local copies, waits for them, and re-layouts, shards(): part = lax.dynamic_index_in_dim(parts, mine ^ mask, 0, keepdims=False)  7.65 us
    transpose x1, local copies, waits for them, and re-layouts, shards(): core.reshape(cx_local, comps * cy_local, n_gx, share).transpose(2, 0, 1, 3)  5.14 us
    reshape x1, local copies, waits for them, and re-layouts, shards(): core.reshape(cx_local, comps * cy_local, n_gx, share).transpose(2, 0, 1, 3)  4.52 us
  transfers between devices with their start and end apart: 19, of which 17 were waited for; matrix products, arithmetic and copies ran while one was open for 5% of the time, Pallas kernels for 0%

profile of v2, /device:TPU:0, one launch (start us, length us, event | category | flops | bytes accessed | tf_op | source)
XLA Modules:
  0.0 182.8 jit_solution(3845638483338370209)
XLA Ops:
  0.6 11.7 %fusion.5 = f32[512,512]{1,0:T(8,128)S(1)} fusion(f32[96,16,3,512]{3,1,2,0:T(8,128)} %param.3), kind=kOutput, calls=%fused_computation.4 | convolution fusion | flops 7248019456 | bytes 10485760 | tf_op jit(solution)/shard_map/dot_general | solution.py:151
  14.4 3.0 %collective-permute-start.1 = (f32[320,128]{1,0:T(8,128)S(1)}, f32[320,128]{1,0:T(8,128)S(1)}, u32[]{:S(2)}, u32[]{:S(2)}) collective-permute-start(f32[320,128]{1,0:T(8,128)S(1)} %slice_select_fusion), channel_id=1, source_target_pairs={{0,16},{8,24},{16,0},{24,8},{1,17},{9,25},{17,1},{25,9},{2,18},{10... | collective-permute-start | bytes 491528 | tf_op jit(solution)/shard_map/ppermute | solution.py:104
  17.3 4.5 %collective-permute-done.1 = f32[320,128]{1,0:T(8,128)S(1)} collective-permute-done((f32[320,128]{1,0:T(8,128)S(1)}, f32[320,128]{1,0:T(8,128)S(1)}, u32[]{:S(2)}, u32[]{:S(2)}) %collective-permute-start.1) | collective-permute-done | bytes 163872 | tf_op jit(solution)/shard_map/ppermute | solution.py:104
  23.6 2.7 %collective-permute-done.2 = f32[160,128]{1,0:T(8,128)S(1)} collective-permute-done((f32[160,128]{1,0:T(8,128)S(1)}, f32[160,128]{1,0:T(8,128)S(1)}, u32[]{:S(2)}, u32[]{:S(2)}) %collective-permute-start.2) | collective-permute-done | bytes 81952 | tf_op jit(solution)/shard_map/ppermute | solution.py:104
  28.2 2.6 %collective-permute-done.3 = f32[160,128]{1,0:T(8,128)S(1)} collective-permute-done((f32[160,128]{1,0:T(8,128)S(1)}, f32[160,128]{1,0:T(8,128)S(1)}, u32[]{:S(2)}, u32[]{:S(2)}) %collective-permute-start.3) | collective-permute-done | bytes 81952 | tf_op jit(solution)/shard_map/ppermute | solution.py:104
  30.9 3.4 %collective-permute-start.4 = (f32[160,128]{1,0:T(8,128)S(1)}, f32[160,128]{1,0:T(8,128)S(1)}, u32[]{:S(2)}, u32[]{:S(2)}) collective-permute-start(f32[160,128]{1,0:T(8,128)S(1)} %add.51), channel_id=1, source_target_pairs={{0,4},{1,5},{2,6},{3,7},{4,0},{5,1},{6,2},{7,3},{8,12},{9,13},{10,... | collective-permute-start | bytes 245768 | tf_op jit(solution)/shard_map/ppermute | solution.py:104
  34.3 2.4 %collective-permute-done.4 = f32[160,128]{1,0:T(8,128)S(1)} collective-permute-done((f32[160,128]{1,0:T(8,128)S(1)}, f32[160,128]{1,0:T(8,128)S(1)}, u32[]{:S(2)}, u32[]{:S(2)}) %collective-permute-start.4) | collective-permute-done | bytes 81952 | tf_op jit(solution)/shard_map/ppermute | solution.py:104
  38.3 3.0 %collective-permute-done.5 = f32[160,128]{1,0:T(8,128)S(1)} collective-permute-done((f32[160,128]{1,0:T(8,128)S(1)}, f32[160,128]{1,0:T(8,128)S(1)}, u32[]{:S(2)}, u32[]{:S(2)}) %collective-permute-start.5) | collective-permute-done | bytes 81952 | tf_op jit(solution)/shard_map/ppermute | solution.py:104
  42.9 3.8 %collective-permute-done.6 = f32[320,128]{1,0:T(8,128)S(1)} collective-permute-done((f32[320,128]{1,0:T(8,128)S(1)}, f32[320,128]{1,0:T(8,128)S(1)}, u32[]{:S(2)}, u32[]{:S(2)}) %collective-permute-start.6) | collective-permute-done | bytes 163872 | tf_op jit(solution)/shard_map/ppermute | solution.py:104
  48.4 21.1 %leading_basis.2 = f32[128,512]{1,0:T(8,128)S(1)} custom-call(f32[1280,128]{1,0:T(8,128)S(1)} %maximum_select_fusion.packed_ref, f32[512,128]{1,0:T(8,128)S(1)} %copy-done), custom_call_target="tpu_custom_call" | custom-call | tf_op jit(solution)/shard_map/leading_basis/pallas_call | solution.py:85
  69.5 8.4 %convolution_bitcast_fusion = f32[4608,128]{0,1:T(8,128)S(1)} fusion(f32[128,512]{1,0:T(8,128)S(1)} %leading_basis.2, f32[4608,512]{1,0:T(8,128)} %bitcast.53), kind=kOutput, calls=%fused_computation.2 | convolution fusion | flops 1811939328 | bytes 12058624 | tf_op jit(solution)/shard_map/dot_general | solution.py:158
  78.0 4.5 %reshape.23 = f32[96,48,4,32]{1,0,3,2:T(8,128)} reshape(f32[4608,128]{0,1:T(8,128)S(1)} %convolution_bitcast_fusion) | data formatting | bytes 4718592 | tf_op jit(solution)/shard_map/reshape | solution.py:162
  82.5 5.1 %copy.17 = f32[4,96,48,32]{1,3,2,0:T(8,128)S(1)} copy(f32[4,96,48,32]{2,1,3,0:T(8,128)} %bitcast.51) | data formatting | bytes 4718592 | tf_op jit(solution)/shard_map/transpose | solution.py:162
  97.6 13.3 %collective-permute-done.9 = f32[96,1536]{1,0:T(8,128)} collective-permute-done((f32[96,1536]{1,0:T(8,128)}, f32[96,1536]{1,0:T(8,128)}, u32[]{:S(2)}, u32[]{:S(2)}) %collective-permute-start.9) | collective-permute-done | bytes 589856 | tf_op jit(solution)/shard_map/ppermute | solution.py:104
  112.0 10.3 %collective-permute-done.10 = f32[96,1536]{1,0:T(8,128)S(1)} collective-permute-done((f32[96,1536]{1,0:T(8,128)}, f32[96,1536]{1,0:T(8,128)S(1)}, u32[]{:S(2)}, u32[]{:S(2)}) %collective-permute-start.10) | collective-permute-done | bytes 589856 | tf_op jit(solution)/shard_map/ppermute | solution.py:104
  127.6 3.5 %collective-permute-done.12 = f32[192,128]{1,0:T(8,128)S(1)} collective-permute-done((f32[192,128]{1,0:T(8,128)S(1)}, f32[192,128]{1,0:T(8,128)S(1)}, u32[]{:S(2)}, u32[]{:S(2)}) %collective-permute-start.12) | collective-permute-done | bytes 98336 | tf_op jit(solution)/shard_map/ppermute | solution.py:104
  132.7 2.6 %collective-permute-done.13 = f32[96,128]{1,0:T(8,128)S(1)} collective-permute-done((f32[96,128]{1,0:T(8,128)S(1)}, f32[96,128]{1,0:T(8,128)S(1)}, u32[]{:S(2)}, u32[]{:S(2)}) %collective-permute-start.13) | collective-permute-done | bytes 49184 | tf_op jit(solution)/shard_map/ppermute | solution.py:104
  136.9 2.6 %collective-permute-done.14 = f32[96,128]{1,0:T(8,128)S(1)} collective-permute-done((f32[96,128]{1,0:T(8,128)S(1)}, f32[96,128]{1,0:T(8,128)S(1)}, u32[]{:S(2)}, u32[]{:S(2)}) %collective-permute-start.14) | collective-permute-done | bytes 49184 | tf_op jit(solution)/shard_map/ppermute | solution.py:104
  139.5 3.1 %collective-permute-start.15 = (f32[96,128]{1,0:T(8,128)S(1)}, f32[96,128]{1,0:T(8,128)S(1)}, u32[]{:S(2)}, u32[]{:S(2)}) collective-permute-start(f32[96,128]{1,0:T(8,128)S(1)} %add.60), channel_id=1, source_target_pairs={{0,4},{1,5},{2,6},{3,7},{4,0},{5,1},{6,2},{7,3},{8,12},{9,13},{10,... | collective-permute-start | bytes 147464 | tf_op jit(solution)/shard_map/ppermute | solution.py:104
  146.2 2.6 %collective-permute-done.16 = f32[96,128]{1,0:T(8,128)S(1)} collective-permute-done((f32[96,128]{1,0:T(8,128)S(1)}, f32[96,128]{1,0:T(8,128)S(1)}, u32[]{:S(2)}, u32[]{:S(2)}) %collective-permute-start.16) | collective-permute-done | bytes 49184 | tf_op jit(solution)/shard_map/ppermute | solution.py:104
  150.4 3.1 %collective-permute-done.17 = f32[192,128]{1,0:T(8,128)S(1)} collective-permute-done((f32[192,128]{1,0:T(8,128)S(1)}, f32[192,128]{1,0:T(8,128)S(1)}, u32[]{:S(2)}, u32[]{:S(2)}) %collective-permute-start.17) | collective-permute-done | bytes 98336 | tf_op jit(solution)/shard_map/ppermute | solution.py:104
  153.6 3.0 %copy.16 = f32[4608,128]{1,0:T(8,128)} copy(f32[4608,128]{0,1:T(8,128)} %copy-done.2) | data formatting | bytes 4718592 | tf_op jit(solution)/shard_map/dot_general | solution.py:158
  158.7 20.4 %leading_basis.3 = f32[128,384]{1,0:T(8,128)S(1)} custom-call(f32[768,128]{1,0:T(8,128)S(1)} %maximum_select_fusion.1.packed_ref, f32[384,128]{1,0:T(8,128)S(1)} %copy-done.1), custom_call_target="tpu_custom_call" | custom-call | tf_op jit(solution)/shard_map/leading_basis/pallas_call | solution.py:85
  179.1 2.8 %convolution_bitcast_fusion.1 = f32[16,3,32,128]{3,2,0,1:T(8,128)S(1)} fusion(f32[3,16,32,384]{3,2,1,0:T(8,128)} %bitcast.54, f32[128,384]{1,0:T(8,128)S(1)} %leading_basis.3), kind=kOutput, calls=%fused_computation.5 | convolution fusion | flops 452984832 | bytes 3342336 | tf_op jit(solution)/shard_map/dot_general | solution.py:177
  (75 shorter events, 38.2 us)
Async XLA Ops:
  12.5 1.8 collective-permute-start
  14.3 34.1 %copy-start = (f32[512,128]{1,0:T(8,128)S(1)}, f32[512,128]{1,0:T(8,128)}, u32[]{:S(2)}) copy-start(f32[512,128]{1,0:T(8,128)} %sketch_ref.2) | copy-start | bytes 786436
  14.4 7.5 %collective-permute-start.1 = (f32[320,128]{1,0:T(8,128)S(1)}, f32[320,128]{1,0:T(8,128)S(1)}, u32[]{:S(2)}, u32[]{:S(2)}) collective-permute-start(f32[320,128]{1,0:T(8,128)S(1)} %slice_select_fusion), channel_id=1, source_target_pairs={{0,16},{8,24},{16,0},{24,8},{1,17},{9,25},{17,1},{25,9},{2,18},{10... | collective-permute-start | bytes 491528 | tf_op jit(solution)/shard_map/ppermute | solution.py:104
  21.9 4.5 %collective-permute-start.2 = (f32[160,128]{1,0:T(8,128)S(1)}, f32[160,128]{1,0:T(8,128)S(1)}, u32[]{:S(2)}, u32[]{:S(2)}) collective-permute-start(f32[160,128]{1,0:T(8,128)S(1)} %slice_select_fusion.2), channel_id=1, source_target_pairs={{0,1},{1,0},{2,3},{3,2},{4,5},{5,4},{6,7},{7,6},{8,9},{9,8},{10,11... | collective-permute-start | bytes 245768 | tf_op jit(solution)/shard_map/ppermute | solution.py:104
  26.4 4.5 %collective-permute-start.3 = (f32[160,128]{1,0:T(8,128)S(1)}, f32[160,128]{1,0:T(8,128)S(1)}, u32[]{:S(2)}, u32[]{:S(2)}) collective-permute-start(f32[160,128]{1,0:T(8,128)S(1)} %select_add_fusion.4), channel_id=1, source_target_pairs={{0,2},{1,3},{2,0},{3,1},{4,6},{5,7},{6,4},{7,5},{8,10},{9,11},{10,... | collective-permute-start | bytes 245768 | tf_op jit(solution)/shard_map/ppermute | solution.py:104
  30.9 5.8 %collective-permute-start.4 = (f32[160,128]{1,0:T(8,128)S(1)}, f32[160,128]{1,0:T(8,128)S(1)}, u32[]{:S(2)}, u32[]{:S(2)}) collective-permute-start(f32[160,128]{1,0:T(8,128)S(1)} %add.51), channel_id=1, source_target_pairs={{0,4},{1,5},{2,6},{3,7},{4,0},{5,1},{6,2},{7,3},{8,12},{9,13},{10,... | collective-permute-start | bytes 245768 | tf_op jit(solution)/shard_map/ppermute | solution.py:104
  36.7 4.5 %collective-permute-start.5 = (f32[160,128]{1,0:T(8,128)S(1)}, f32[160,128]{1,0:T(8,128)S(1)}, u32[]{:S(2)}, u32[]{:S(2)}) collective-permute-start(f32[160,128]{1,0:T(8,128)S(1)} %add.52), channel_id=1, source_target_pairs={{0,1},{1,0},{2,3},{3,2},{4,5},{5,4},{6,7},{7,6},{8,9},{9,8},{10,11... | collective-permute-start | bytes 245768 | tf_op jit(solution)/shard_map/ppermute | solution.py:104
  41.3 5.4 %collective-permute-start.6 = (f32[320,128]{1,0:T(8,128)S(1)}, f32[320,128]{1,0:T(8,128)S(1)}, u32[]{:S(2)}, u32[]{:S(2)}) collective-permute-start(f32[320,128]{1,0:T(8,128)S(1)} %maximum_select_fusion.4), channel_id=1, source_target_pairs={{0,16},{8,24},{16,0},{24,8},{1,17},{9,25},{17,1},{25,9},{2,18},{10... | collective-permute-start | bytes 491528 | tf_op jit(solution)/shard_map/ppermute | solution.py:104
  46.7 1.7 collective-permute-start.7
  78.0 4.5 %copy-start.2 = (f32[4608,128]{0,1:T(8,128)}, f32[4608,128]{0,1:T(8,128)S(1)}, u32[]{:S(2)}) copy-start(f32[4608,128]{0,1:T(8,128)S(1)} %convolution_bitcast_fusion) | copy-start | bytes 7077892
  89.4 3.9 %copy-start.4 = (f32[1,96,1536]{1,2,0:T(8,128)S(1)}, f32[1,96,1536]{1,2,0:T(8,128)}, u32[]{:S(2)}) copy-start(f32[1,96,1536]{1,2,0:T(8,128)} %get-tuple-element.9) | copy-start | bytes 1769476
  89.4 6.5 %copy-start.3 = (f32[1,96,1536]{1,2,0:T(8,128)S(1)}, f32[1,96,1536]{1,2,0:T(8,128)}, u32[]{:S(2)}) copy-start(f32[1,96,1536]{1,2,0:T(8,128)} %get-tuple-element.8) | copy-start | bytes 1769476
  91.8 5.8 %collective-permute-start.8 = (f32[96,1536]{1,0:T(8,128)}, f32[96,1536]{1,0:T(8,128)S(1)}, u32[]{:S(2)}, u32[]{:S(2)}) collective-permute-start(f32[96,1536]{1,0:T(8,128)} %bitcast.9), channel_id=1, source_target_pairs={{0,8},{8,0},{16,24},{24,16},{1,9},{9,1},{17,25},{25,17},{2,10},{10... | collective-permute-start | bytes 1769480 | tf_op jit(solution)/shard_map/ppermute | solution.py:104
  94.4 16.5 %collective-permute-start.9 = (f32[96,1536]{1,0:T(8,128)}, f32[96,1536]{1,0:T(8,128)}, u32[]{:S(2)}, u32[]{:S(2)}) collective-permute-start(f32[96,1536]{1,0:T(8,128)} %bitcast.11), channel_id=1, source_target_pairs={{0,16},{8,24},{16,0},{24,8},{1,17},{9,25},{17,1},{25,9},{2,18},{10... | collective-permute-start | bytes 1769480 | tf_op jit(solution)/shard_map/ppermute | solution.py:104
  97.0 25.3 %collective-permute-start.10 = (f32[96,1536]{1,0:T(8,128)}, f32[96,1536]{1,0:T(8,128)S(1)}, u32[]{:S(2)}, u32[]{:S(2)}) collective-permute-start(f32[96,1536]{1,0:T(8,128)} %bitcast.13), channel_id=1, source_target_pairs={{0,24},{8,16},{16,8},{24,0},{1,25},{9,17},{17,9},{25,1},{2,26},{10... | collective-permute-start | bytes 1769480 | tf_op jit(solution)/shard_map/ppermute | solution.py:104
  124.4 1.5 collective-permute-start.11
  126.0 5.1 %collective-permute-start.12 = (f32[192,128]{1,0:T(8,128)S(1)}, f32[192,128]{1,0:T(8,128)S(1)}, u32[]{:S(2)}, u32[]{:S(2)}) collective-permute-start(f32[192,128]{1,0:T(8,128)S(1)} %slice_select_fusion.1), channel_id=1, source_target_pairs={{0,16},{8,24},{16,0},{24,8},{1,17},{9,25},{17,1},{25,9},{2,18},{10... | collective-permute-start | bytes 294920 | tf_op jit(solution)/shard_map/ppermute | solution.py:104
  131.2 4.2 %collective-permute-start.13 = (f32[96,128]{1,0:T(8,128)S(1)}, f32[96,128]{1,0:T(8,128)S(1)}, u32[]{:S(2)}, u32[]{:S(2)}) collective-permute-start(f32[96,128]{1,0:T(8,128)S(1)} %slice_select_fusion.3), channel_id=1, source_target_pairs={{0,1},{1,0},{2,3},{3,2},{4,5},{5,4},{6,7},{7,6},{8,9},{9,8},{10,11... | collective-permute-start | bytes 147464 | tf_op jit(solution)/shard_map/ppermute | solution.py:104
  135.3 4.2 %collective-permute-start.14 = (f32[96,128]{1,0:T(8,128)S(1)}, f32[96,128]{1,0:T(8,128)S(1)}, u32[]{:S(2)}, u32[]{:S(2)}) collective-permute-start(f32[96,128]{1,0:T(8,128)S(1)} %select_add_fusion.5), channel_id=1, source_target_pairs={{0,2},{1,3},{2,0},{3,1},{4,6},{5,7},{6,4},{7,5},{8,10},{9,11},{10,... | collective-permute-start | bytes 147464 | tf_op jit(solution)/shard_map/ppermute | solution.py:104
  139.5 5.1 %collective-permute-start.15 = (f32[96,128]{1,0:T(8,128)S(1)}, f32[96,128]{1,0:T(8,128)S(1)}, u32[]{:S(2)}, u32[]{:S(2)}) collective-permute-start(f32[96,128]{1,0:T(8,128)S(1)} %add.60), channel_id=1, source_target_pairs={{0,4},{1,5},{2,6},{3,7},{4,0},{5,1},{6,2},{7,3},{8,12},{9,13},{10,... | collective-permute-start | bytes 147464 | tf_op jit(solution)/shard_map/ppermute | solution.py:104
  144.6 4.2 %collective-permute-start.16 = (f32[96,128]{1,0:T(8,128)S(1)}, f32[96,128]{1,0:T(8,128)S(1)}, u32[]{:S(2)}, u32[]{:S(2)}) collective-permute-start(f32[96,128]{1,0:T(8,128)S(1)} %add.61), channel_id=1, source_target_pairs={{0,1},{1,0},{2,3},{3,2},{4,5},{5,4},{6,7},{7,6},{8,9},{9,8},{10,11... | collective-permute-start | bytes 147464 | tf_op jit(solution)/shard_map/ppermute | solution.py:104
  148.8 4.7 %collective-permute-start.17 = (f32[192,128]{1,0:T(8,128)S(1)}, f32[192,128]{1,0:T(8,128)S(1)}, u32[]{:S(2)}, u32[]{:S(2)}) collective-permute-start(f32[192,128]{1,0:T(8,128)S(1)} %maximum_select_fusion.5), channel_id=1, source_target_pairs={{0,16},{8,24},{16,0},{24,8},{1,17},{9,25},{17,1},{25,9},{2,18},{10... | collective-permute-start | bytes 294920 | tf_op jit(solution)/shard_map/ppermute | solution.py:104
  153.5 5.1 %collective-permute-start.18 = (f32[384,128]{1,0:T(8,128)S(1)}, f32[384,128]{1,0:T(8,128)S(1)}, u32[]{:S(2)}, u32[]{:S(2)}) collective-permute-start(f32[384,128]{1,0:T(8,128)S(1)} %maximum_select_fusion.3), channel_id=1, source_target_pairs={{0,8},{8,0},{16,24},{24,16},{1,9},{9,1},{17,25},{25,17},{2,10},{10... | collective-permute-start | bytes 589832 | tf_op jit(solution)/shard_map/ppermute | solution.py:104
  156.6 2.0 %copy-start.1 = (f32[384,128]{1,0:T(8,128)S(1)}, f32[384,128]{1,0:T(8,128)}, u32[]{:S(2)}) copy-start(f32[384,128]{1,0:T(8,128)} %sketch_ref.3) | copy-start | bytes 589828

commit v3 on v2

--- a/solution.py
+++ b/solution.py
@@ -5,11 +5,12 @@
 from jax.experimental.pallas import tpu as pltpu
 from jax.sharding import PartitionSpec as P
 
-HIGH = lax.Precision.HIGH
 BLOCK = 128
 PANEL = 16
 POWER = 3
 HIGHEST = lax.Precision.HIGHEST
+VMEM = pl.BlockSpec(memory_space=pltpu.VMEM)
+LIMIT = pltpu.CompilerParams(vmem_limit_bytes=40 * 2**20)
 
 
 def dot(a, b, ca, cb):
@@ -99,86 +100,247 @@
     )(packed, sketch)
 
 
-def exchange(value, axis, mask):
-    size = lax.axis_size(axis)
-    return lax.ppermute(value, axis, [(i, i ^ mask) for i in range(size)])
-
-
-def bits_of(size):
-    bits = []
-    mask = 1
-    while mask < size:
-        bits.append(mask)
-        mask *= 2
-    return bits
+def split(value):
+    high = value.astype(jnp.bfloat16)
+    return high, (value - high.astype(jnp.float32)).astype(jnp.bfloat16)
+
+
+def pass_dot(a, b, ca, cb):
+    return lax.dot_general(a, b, (((ca,), (cb,)), ((), ())), preferred_element_type=jnp.float32)
+
+
+def pack_triangle(square, cross, out_ref, scale):
+    n = square.shape[0] // BLOCK
+    at = 0
+    for i in range(n):
+        for j in range(i, n):
+            rows, cols = pl.ds(i * BLOCK, BLOCK), pl.ds(j * BLOCK, BLOCK)
+            total = square[rows, cols] + (cross[rows, cols] + cross[cols, rows].T)
+            out_ref[at * BLOCK : (at + 1) * BLOCK, :] = total * scale
+            at += 1
+
+
+def packed_rows(size):
+    n = size // BLOCK
+    return n * (n + 1) // 2 * BLOCK
+
+
+def time_gram(flat, scale):
+    rows, steps = flat.shape
+    block = rows // 6
+    half = steps // 2
+
+    def kernel(flat_ref, out_ref, square, cross):
+        at = pl.program_id(0)
+
+        @pl.when(at == 0)
+        def _():
+            square[...] = jnp.zeros_like(square)
+            cross[...] = jnp.zeros_like(cross)
+
+        high, low = split(flat_ref[...])
+        for i in range(2):
+            here = slice(i * half, (i + 1) * half)
+            square[here, i * half :] += pass_dot(high[:, here], high[:, i * half :], 0, 0)
+            cross[here, :] += pass_dot(high[:, here], low, 0, 0)
+
+        @pl.when(at == pl.num_programs(0) - 1)
+        def _():
+            pack_triangle(square, cross, out_ref, scale)
+
+    return pl.pallas_call(
+        kernel,
+        grid=(6,),
+        out_shape=jax.ShapeDtypeStruct((packed_rows(steps), BLOCK), jnp.float32),
+        in_specs=[pl.BlockSpec((block, steps), lambda i: (i, 0))],
+        out_specs=pl.BlockSpec((packed_rows(steps), BLOCK), lambda i: (0, 0)),
+        scratch_shapes=[pltpu.VMEM((steps, steps), jnp.float32)] * 2,
+        compiler_params=LIMIT,
+        name="time_gram",
+    )(flat)
+
+
+def project(flat, basis, n_gx):
+    sites, inner, steps = flat.shape
+    ranks = basis.shape[0]
+    share = ranks // n_gx
+    groups = inner // n_gx
+    block = 16
+    columns = inner * share
+
+    def kernel(flat_ref, basis_ref, core_ref, *rest):
+        part_refs, (core, parts) = rest[:n_gx], rest[n_gx:]
+        high, low = split(flat_ref[...].reshape(block * inner, steps))
+        basis_high, basis_low = split(basis_ref[...])
+        wide = pass_dot(high, jnp.concatenate([basis_high, basis_low]), 1, 1)
+        value = wide[:, :ranks] + (wide[:, ranks:] + pass_dot(low, basis_high, 1, 1))
+        core[...] = value
+        core_ref[...] = value.reshape(block, inner, ranks)
+        lane = lax.broadcasted_iota(jnp.int32, (block, ranks), 1) // share
+        for group in range(groups):
+            rows = [
+                core[pl.ds(group * n_gx + y, block, stride=inner), :] for y in range(n_gx)
+            ]
+            for owner in range(n_gx):
+                out = rows[owner]
+                for y in range(n_gx):
+                    if y != owner:
+                        moved = pltpu.roll(rows[y], (y - owner) % n_gx * share, 1)
+                        out = jnp.where(lane == y, moved, out)
+                parts[owner, :, group * ranks : (group + 1) * ranks] = out
+        mine = lax.axis_index("gx")
+        for mask in range(n_gx):
+            part_refs[mask][...] = parts[mine ^ mask]
+
+    part = jax.ShapeDtypeStruct((sites, columns), jnp.float32)
+    return pl.pallas_call(
+        kernel,
+        grid=(sites // block,),
+        out_shape=[jax.ShapeDtypeStruct((sites, inner, ranks), jnp.float32)] + [part] * n_gx,
+        in_specs=[
+            pl.BlockSpec((block, inner, steps), lambda i: (i, 0, 0)),
+            pl.BlockSpec((ranks, steps), lambda i: (0, 0)),
+        ],
+        out_specs=[pl.BlockSpec((block, inner, ranks), lambda i: (i, 0, 0))]
+        + [pl.BlockSpec((block, columns), lambda i: (i, 0))] * n_gx,
+        scratch_shapes=[
+            pltpu.VMEM((block * inner, ranks), jnp.float32),
+            pltpu.VMEM((n_gx, block, columns), jnp.float32),
+        ],
+        compiler_params=LIMIT,
+        name="project_time",
+    )(flat, basis)
+
+
+def x_gram(parts, scale):
+    n_gx = len(parts)
+    sites, columns = parts[0].shape
+    size = n_gx * sites
+
+    def kernel(*refs):
+        part_refs = refs[:n_gx]
+        cols_ref, out_ref, square, cross, sems = refs[n_gx:]
+        mine = lax.axis_index("gx")
+        copies = []
+        for mask in range(n_gx):
+            rows = pl.ds(pl.multiple_of((mine ^ mask) * sites, 8), sites)
+            copies.append(
+                pltpu.make_async_copy(part_refs[mask], cols_ref.at[rows, :], sems.at[mask])
+            )
+            copies[-1].start()
+        for copy in copies:
+            copy.wait()
+        high, low = split(cols_ref[...])
+        square[...] = pass_dot(high, high, 1, 1)
+        cross[...] = pass_dot(high, low, 1, 1)
+        pack_triangle(square, cross, out_ref, scale)
+
+    return pl.pallas_call(
+        kernel,
+        out_shape=[
+            jax.ShapeDtypeStruct((size, columns), jnp.float32),
+            jax.ShapeDtypeStruct((packed_rows(size), BLOCK), jnp.float32),
+        ],
+        in_specs=[pl.BlockSpec(memory_space=pl.ANY)] * n_gx,
+        out_specs=[VMEM, VMEM],
+        scratch_shapes=[pltpu.VMEM((size, size), jnp.float32)] * 2
+        + [pltpu.SemaphoreType.DMA((n_gx,))],
+        compiler_params=LIMIT,
+        name="x_gram",
+    )(*parts)
+
+
+def project_x(cols, basis, comps, cy_local, share):
+    ranks = basis.shape[0]
+    per_block = BLOCK // share
+    blocks = cy_local // per_block
+
+    def kernel(cols_ref, basis_ref, out_ref):
+        high, low = split(cols_ref[...])
+        basis_high, basis_low = split(basis_ref[...])
+        value = pass_dot(basis_high, high, 1, 0) + (
+            pass_dot(basis_high, low, 1, 0) + pass_dot(basis_low, high, 1, 0)
+        )
+        for c in range(comps):
+            for b in range(blocks):
+                at = (c * blocks + b) * BLOCK
+                tile = value[:, at : at + BLOCK].T.reshape(per_block, share, ranks)
+                out_ref[b * per_block : (b + 1) * per_block, c] = tile
+
+    return pl.pallas_call(
+        kernel,
+        out_shape=jax.ShapeDtypeStruct((cy_local, comps, share, ranks), jnp.float32),
+        in_specs=[VMEM, VMEM],
+        out_specs=VMEM,
+        compiler_params=LIMIT,
+        name="project_x",
+    )(cols, basis)
+
+
+AXES = ("gx", "gy")
+
+
+def combos(masks):
+    found = [0]
+    for mask in masks:
+        found += [mask ^ old for old in found]
+    return found
+
+
+def exchange(value, mask):
+    size = lax.axis_size(AXES)
+    return lax.ppermute(value, AXES, [(i, i ^ mask) for i in range(size)])
 
 
 def sum_all(buf):
-    steps = [("gx", m) for m in bits_of(lax.axis_size("gx"))]
-    steps += [("gy", m) for m in bits_of(lax.axis_size("gy"))]
-    halved = []
-    for axis, mask in steps:
-        rows = buf.shape[0]
-        if rows % 16 or rows <= 160:
-            buf = buf + exchange(buf, axis, mask)
-            continue
-        upper = (lax.axis_index(axis) & mask) != 0
-        low, high = buf[: rows // 2], buf[rows // 2 :]
-        got = exchange(jnp.where(upper, low, high), axis, mask)
-        buf = jnp.where(upper, high, low) + got
-        halved.append((axis, mask, upper))
-    for axis, mask, upper in reversed(halved):
-        got = exchange(buf, axis, mask)
-        buf = jnp.where(upper, jnp.concatenate([got, buf]), jnp.concatenate([buf, got]))
+    n_gx, n_gy = lax.axis_size("gx"), lax.axis_size("gy")
+    me = lax.axis_index("gx") * n_gy + lax.axis_index("gy")
+    bits = [1 << b for b in range((n_gx * n_gy).bit_length() - 1)]
+    groups = [[n_gy], [1, 2 * n_gy]]
+    later = [m for m in bits if m not in (n_gy, 1, 2 * n_gy)]
+    shared = []
+    for group in groups:
+        masks = combos(group)
+        rows = buf.shape[0] // len(masks)
+        place = sum(jnp.where(me & m, 1 << b, 0) for b, m in enumerate(group))
+        total = lax.dynamic_slice_in_dim(buf, place * rows, rows)
+        for b, mask in enumerate(masks):
+            if b:
+                total = total + exchange(
+                    lax.dynamic_slice_in_dim(buf, (place ^ b) * rows, rows), mask
+                )
+        shared.append((masks, place, rows))
+        buf = total
+    for mask in later:
+        buf = buf + exchange(buf, mask)
+    for masks, place, rows in reversed(shared):
+        whole = jnp.zeros((rows * len(masks), buf.shape[1]), buf.dtype)
+        for b, mask in enumerate(masks):
+            piece = exchange(buf, mask) if b else buf
+            whole = lax.dynamic_update_slice_in_dim(whole, piece, (place ^ b) * rows, 0)
+        buf = whole
     return buf
-
-
-def sum_gram(partial):
-    n = partial.shape[0] // BLOCK
-    pairs = [(i, j) for i in range(n) for j in range(i, n)]
-
-    def block(i, j):
-        return partial[i * BLOCK : (i + 1) * BLOCK, j * BLOCK : (j + 1) * BLOCK]
-
-    return sum_all(jnp.concatenate([block(i, j) for i, j in pairs]))
 
 
 def shards(motion, time_sketch, x_sketch):
     cx_local, cy_local, comps, steps = motion.shape
     n_gx = lax.axis_size("gx")
     n_gy = lax.axis_size("gy")
-    flat = motion.transpose(0, 2, 1, 3).reshape(cx_local * comps * cy_local, steps)
-    partial_value = lax.dot_general(
-        flat, flat, (((0,), (0,)), ((), ())), precision=HIGH, preferred_element_type=jnp.float32
-    )
-    partial_value = partial_value / (cx_local * n_gx * cy_local * n_gy * comps)
-    time_basis = leading_basis(sum_gram(partial_value), time_sketch)
-    ranks = time_basis.shape[0]
+    ranks = time_sketch.shape[1]
     share = ranks // n_gx
-    core = jnp.dot(flat, time_basis.T, precision=HIGH, preferred_element_type=jnp.float32)
+    inner = comps * cy_local
+    flat = motion.transpose(0, 2, 1, 3).reshape(cx_local, inner, steps)
+
+    scale = 1.0 / (cx_local * n_gx * cy_local * n_gy * comps)
+    packed = time_gram(flat.reshape(cx_local * inner, steps), scale)
+    time_basis = leading_basis(sum_all(packed), time_sketch)
+    core, *parts = project(flat, time_basis, n_gx)
     time_core = core.reshape(cx_local, comps, cy_local, ranks).transpose(0, 2, 1, 3)
 
-    columns = comps * cy_local * share
-    parts = core.reshape(cx_local, comps * cy_local, n_gx, share).transpose(2, 0, 1, 3)
-    parts = parts.reshape(n_gx, cx_local, columns)
-    mine = lax.axis_index("gx")
-    cols = jnp.zeros((n_gx, cx_local, columns), jnp.float32)
-    for mask in range(n_gx):
-        part = lax.dynamic_index_in_dim(parts, mine ^ mask, 0, keepdims=False)
-        if mask:
-            part = exchange(part, "gx", mask)
-        cols = lax.dynamic_update_index_in_dim(cols, part, mine ^ mask, 0)
-    cols = cols.reshape(n_gx * cx_local, columns)
-
-    x_partial = jnp.dot(cols, cols.T, precision=HIGH, preferred_element_type=jnp.float32) / (
-        cy_local * n_gy * comps * ranks
-    )
-    x_basis = leading_basis(sum_gram(x_partial), x_sketch)
-    x_core = lax.dot_general(
-        cols, x_basis, (((0,), (1,)), ((), ())), precision=HIGH, preferred_element_type=jnp.float32
-    )
-    x_core = x_core.reshape(comps, cy_local, share, x_basis.shape[0]).transpose(1, 0, 2, 3)
-    return (time_core, x_core)
+    parts = [exchange(part, mask * n_gy) if mask else part for mask, part in enumerate(parts)]
+    cols, packed = x_gram(parts, 1.0 / (cy_local * n_gy * comps * ranks))
+    x_basis = leading_basis(sum_all(packed), x_sketch)
+    return (time_core, project_x(cols, x_basis, comps, cy_local, share))
 
 
 def solution(mesh):

time: 183 us -> 155 us (0.85)
  matrix products: 24.9 us -> 0 us
  Pallas kernels: 41.5 us -> 57.9 us
  local copies, waits for them, and re-layouts: 24.9 us -> 12.2 us
  waiting for transfers between devices: 63.1 us -> 55.6 us
    dot_general x4 -> x0, matrix products: 24.9 us -> none  [the longest x1 11.7 us: shards(): lax.dot_general(flat, flat, (((0,), (0,)), ((), ())), precision=HIGH, pre...]
    pallas_call x0 -> x4, Pallas kernels: none -> 16.6 us  [the longest x1 6.75 us: project(): pl.pallas_call(kernel, grid=(sites // block,), out_shape=[jax.ShapeDtypeS...]
    unnamed x15 -> x18, local copies, waits for them, and re-layouts: 1 us -> 11.8 us
    dynamic_slice x5 -> x4, local copies, waits for them, and re-layouts: 7.65 us -> 0.09 us  [sum_all(): lax.dynamic_slice_in_dim(buf, (place ^ b) * rows, rows)]
    ppermute x19 -> x23, waiting for transfers between devices: 63.1 us -> 55.6 us  [exchange(): return lax.ppermute(value, AXES, [(i, i ^ mask) for i in range(size)])]
    transpose x1 -> x0, local copies, waits for them, and re-layouts: 5.14 us -> none  [shards(): core.reshape(cx_local, comps * cy_local, n_gx, share).transpose(2, 0, 1, 3)]
    dot_general x2 -> x0, local copies, waits for them, and re-layouts: 5.04 us -> none  [the longest x1 3.05 us: shards(): jnp.dot(flat, time_basis.T, precision=HIGH, preferred_element_type=jnp.fl...]
    reshape x1 -> x0, local copies, waits for them, and re-layouts: 4.52 us -> none  [shards(): core.reshape(cx_local, comps * cy_local, n_gx, share).transpose(2, 0, 1, 3)]
  transfers between devices with their start and end apart: 19 -> 23, of which waited for: 17 -> 23; matrix products, arithmetic and copies ran while one was open for 5% -> 0% of each run, Pallas kernels for 0% -> 0%
where the time goes in v3:
time: 155 us
  Pallas kernels  57.9 us (37%)
  waiting for transfers between devices  55.6 us (36%)
  starting transfers between devices  27 us (17%)
  local copies, waits for them, and re-layouts  12.2 us (8%)
    ppermute x23, waiting for transfers between devices, exchange(): return lax.ppermute(value, AXES, [(i, i ^ mask) for i in range(size)])  55.6 us
    pallas_call x2, Pallas kernels, leading_basis(): pl.pallas_call(basis_kernel, out_shape=jax.ShapeDtypeStruct((ranks, size)...  41.3 us
    ppermute x23, starting transfers between devices, exchange(): return lax.ppermute(value, AXES, [(i, i ^ mask) for i in range(size)])  27 us
    unnamed x18, local copies, waits for them, and re-layouts  11.8 us
    pallas_call x1, Pallas kernels, project(): pl.pallas_call(kernel, grid=(sites // block,), out_shape=[jax.ShapeDtypeS...  6.75 us
    pallas_call x1, Pallas kernels, time_gram(): pl.pallas_call(kernel, grid=(6,), out_shape=jax.ShapeDtypeStruct((packed_...  6.02 us
  transfers between devices with their start and end apart: 23, of which 23 were waited for; matrix products, arithmetic and copies ran while one was open for 0% of the time, Pallas kernels for 0%

profile of v3, /device:TPU:0, one launch (start us, length us, event | category | flops | bytes accessed | tf_op | source)
XLA Modules:
  0.0 154.7 jit_solution(8037080230448886899)
XLA Ops:
  0.6 3.7 %copy-done = f32[96,16,3,512]{3,1,2,0:T(8,128)S(1)} copy-done((f32[96,16,3,512]{3,1,2,0:T(8,128)S(1)}, f32[96,16,3,512]{3,1,2,0:T(8,128)}, u32[]{:S(2)}) %copy-start) | copy-done | bytes 9437208
  4.3 6.0 %time_gram.1 = f32[1280,128]{1,0:T(8,128)S(1)} custom-call(f32[4608,512]{1,0:T(8,128)S(1)} %bitcast.8), custom_call_target="tpu_custom_call" | custom-call | tf_op jit(solution)/shard_map/time_gram/pallas_call | solution.py:151
  12.3 3.9 %collective-permute-start.3 = (f32[160,128]{1,0:T(8,128)S(1)}, f32[160,128]{1,0:T(8,128)S(1)}, u32[]{:S(2)}, u32[]{:S(2)}) collective-permute-start(f32[160,128]{1,0:T(8,128)S(1)} %get-tuple-element.21), channel_id=1, source_target_pairs={{0,17},{1,16},{2,19},{3,18},{4,21},{5,20},{6,23},{7,22},{8,25},{9,... | collective-permute-start | bytes 245768 | tf_op jit(solution)/shard_map/ppermute | solution.py:292
  16.8 2.2 %collective-permute-done.3 = f32[160,128]{1,0:T(8,128)S(1)} collective-permute-done((f32[160,128]{1,0:T(8,128)S(1)}, f32[160,128]{1,0:T(8,128)S(1)}, u32[]{:S(2)}, u32[]{:S(2)}) %collective-permute-start.3) | collective-permute-done | bytes 81952 | tf_op jit(solution)/shard_map/ppermute | solution.py:292
  19.0 1.7 %collective-permute-done.2 = f32[160,128]{1,0:T(8,128)S(1)} collective-permute-done((f32[160,128]{1,0:T(8,128)S(1)}, f32[160,128]{1,0:T(8,128)S(1)}, u32[]{:S(2)}, u32[]{:S(2)}) %collective-permute-start.2) | collective-permute-done | bytes 81952 | tf_op jit(solution)/shard_map/ppermute | solution.py:292
  21.1 1.6 %collective-permute-start.4 = (f32[160,128]{1,0:T(8,128)S(1)}, f32[160,128]{1,0:T(8,128)S(1)}, u32[]{:S(2)}, u32[]{:S(2)}) collective-permute-start(f32[160,128]{1,0:T(8,128)S(1)} %add_add_fusion), channel_id=1, source_target_pairs={{0,2},{1,3},{2,0},{3,1},{4,6},{5,7},{6,4},{7,5},{8,10},{9,11},{10,... | collective-permute-start | bytes 245768 | tf_op jit(solution)/shard_map/ppermute | solution.py:292
  22.8 2.9 %collective-permute-done.4 = f32[160,128]{1,0:T(8,128)S(1)} collective-permute-done((f32[160,128]{1,0:T(8,128)S(1)}, f32[160,128]{1,0:T(8,128)S(1)}, u32[]{:S(2)}, u32[]{:S(2)}) %collective-permute-start.4) | collective-permute-done | bytes 81952 | tf_op jit(solution)/shard_map/ppermute | solution.py:292
  25.6 2.7 %collective-permute-start.5 = (f32[160,128]{1,0:T(8,128)S(1)}, f32[160,128]{1,0:T(8,128)S(1)}, u32[]{:S(2)}, u32[]{:S(2)}) collective-permute-start(f32[160,128]{1,0:T(8,128)S(1)} %add.104), channel_id=1, source_target_pairs={{0,4},{1,5},{2,6},{3,7},{4,0},{5,1},{6,2},{7,3},{8,12},{9,13},{10,... | collective-permute-start | bytes 245768 | tf_op jit(solution)/shard_map/ppermute | solution.py:292
  28.3 2.7 %collective-permute-done.5 = f32[160,128]{1,0:T(8,128)S(1)} collective-permute-done((f32[160,128]{1,0:T(8,128)S(1)}, f32[160,128]{1,0:T(8,128)S(1)}, u32[]{:S(2)}, u32[]{:S(2)}) %collective-permute-start.5) | collective-permute-done | bytes 81952 | tf_op jit(solution)/shard_map/ppermute | solution.py:292
  36.9 1.6 %collective-permute-done.8 = f32[160,128]{1,0:T(8,128)S(1)} collective-permute-done((f32[160,128]{1,0:T(8,128)S(1)}, f32[160,128]{1,0:T(8,128)S(1)}, u32[]{:S(2)}, u32[]{:S(2)}) %collective-permute-start.8) | collective-permute-done | bytes 81952 | tf_op jit(solution)/shard_map/ppermute | solution.py:292
  40.3 20.9 %leading_basis.2.basis_ref = f32[128,512]{1,0:T(8,128)S(1)} custom-call(f32[1280,128]{1,0:T(8,128)S(1)} %constant_dynamic-update-slice_fusion.6.packed_ref, f32[512,128]{1,0:T(8,128)S(1)} %copy-done.7), custom_call_target="tpu_custom_call" | custom-call | tf_op jit(solution)/shard_map/leading_basis/pallas_call | solution.py:86
  61.2 3.7 %copy-done.1 = f32[96,16,3,512]{3,1,2,0:T(8,128)S(1)} copy-done((f32[96,16,3,512]{3,1,2,0:T(8,128)S(1)}, f32[96,16,3,512]{3,1,2,0:T(8,128)}, u32[]{:S(2)}) %copy-start.1) | copy-done | bytes 9437208
  64.9 6.7 %project_time.1 = (f32[96,48,128]{2,1,0:T(8,128)}, f32[96,1536]{1,0:T(8,128)S(1)}, f32[96,1536]{1,0:T(8,128)}, f32[96,1536]{1,0:T(8,128)S(1)}, f32[96,1536]{1,0:T(8,128)S(1)}) custom-call(f32[96,48,512]{2,1,0:T(8,128)S(1)} %bitcast.9, f32[128,512]{1,0:T(8,128)S(1)} %leading_basis.2.basis_ref), custom_call_target="tpu_custom_call" | custom-call | tf_op jit(solution)/shard_map/project_time/pallas_call | solution.py:196
  73.9 14.1 %collective-permute-done.11.refs_2_ = f32[96,1536]{1,0:T(8,128)S(1)} collective-permute-done((f32[96,1536]{1,0:T(8,128)S(1)}, f32[96,1536]{1,0:T(8,128)S(1)}, u32[]{:S(2)}, u32[]{:S(2)}) %collective-permute-start.11) | collective-permute-done | bytes 589856 | tf_op jit(solution)/shard_map/ppermute | solution.py:292
  88.8 10.7 %collective-permute-done.12.refs_3_ = f32[96,1536]{1,0:T(8,128)S(1)} collective-permute-done((f32[96,1536]{1,0:T(8,128)S(1)}, f32[96,1536]{1,0:T(8,128)S(1)}, u32[]{:S(2)}, u32[]{:S(2)}) %collective-permute-start.12) | collective-permute-done | bytes 589856 | tf_op jit(solution)/shard_map/ppermute | solution.py:292
  102.4 2.0 %x_gram.1 = (f32[384,1536]{1,0:T(8,128)S(1)}, f32[768,128]{1,0:T(8,128)S(1)}) custom-call(f32[96,1536]{1,0:T(8,128)S(1)} %get-tuple-element.10.refs_0_, f32[96,1536]{1,0:T(8,128)S(1)} %collective-permute-done.10.refs_1_, f32[96,1536]{1,0:T(8,128)S(1)} %copy-done.3, f32[96,1536]{1,0:T(8,128)S(1)} %copy-done.5), custom_call_target="tpu_custom_call" | custom-call | tf_op jit(solution)/shard_map/x_gram/pallas_call | solution.py:238
  114.9 1.6 %collective-permute-start.17 = (f32[96,128]{1,0:T(8,128)S(1)}, f32[96,128]{1,0:T(8,128)S(1)}, u32[]{:S(2)}, u32[]{:S(2)}) collective-permute-start(f32[96,128]{1,0:T(8,128)S(1)} %add_add_fusion.1), channel_id=1, source_target_pairs={{0,2},{1,3},{2,0},{3,1},{4,6},{5,7},{6,4},{7,5},{8,10},{9,11},{10,... | collective-permute-start | bytes 147464 | tf_op jit(solution)/shard_map/ppermute | solution.py:292
  116.5 2.5 %collective-permute-done.17 = f32[96,128]{1,0:T(8,128)S(1)} collective-permute-done((f32[96,128]{1,0:T(8,128)S(1)}, f32[96,128]{1,0:T(8,128)S(1)}, u32[]{:S(2)}, u32[]{:S(2)}) %collective-permute-start.17) | collective-permute-done | bytes 49184 | tf_op jit(solution)/shard_map/ppermute | solution.py:292
  119.0 3.0 %collective-permute-start.18 = (f32[96,128]{1,0:T(8,128)S(1)}, f32[96,128]{1,0:T(8,128)S(1)}, u32[]{:S(2)}, u32[]{:S(2)}) collective-permute-start(f32[96,128]{1,0:T(8,128)S(1)} %add.116), channel_id=1, source_target_pairs={{0,4},{1,5},{2,6},{3,7},{4,0},{5,1},{6,2},{7,3},{8,12},{9,13},{10,... | collective-permute-start | bytes 147464 | tf_op jit(solution)/shard_map/ppermute | solution.py:292
  122.0 2.1 %collective-permute-done.18 = f32[96,128]{1,0:T(8,128)S(1)} collective-permute-done((f32[96,128]{1,0:T(8,128)S(1)}, f32[96,128]{1,0:T(8,128)S(1)}, u32[]{:S(2)}, u32[]{:S(2)}) %collective-permute-start.18) | collective-permute-done | bytes 49184 | tf_op jit(solution)/shard_map/ppermute | solution.py:292
  126.0 1.6 %collective-permute-start.21 = (f32[96,128]{1,0:T(8,128)S(1)}, f32[96,128]{1,0:T(8,128)S(1)}, u32[]{:S(2)}, u32[]{:S(2)}) collective-permute-start(f32[96,128]{1,0:T(8,128)S(1)} %get-tuple-element.17), channel_id=1, source_target_pairs={{0,17},{1,16},{2,19},{3,18},{4,21},{5,20},{6,23},{7,22},{8,25},{9,... | collective-permute-start | bytes 147464 | tf_op jit(solution)/shard_map/ppermute | solution.py:292
  128.8 2.2 %collective-permute-done.21 = f32[96,128]{1,0:T(8,128)S(1)} collective-permute-done((f32[96,128]{1,0:T(8,128)S(1)}, f32[96,128]{1,0:T(8,128)S(1)}, u32[]{:S(2)}, u32[]{:S(2)}) %collective-permute-start.21) | collective-permute-done | bytes 49184 | tf_op jit(solution)/shard_map/ppermute | solution.py:292
  132.5 20.4 %leading_basis.3.basis_ref = f32[128,384]{1,0:T(8,128)S(1)} custom-call(f32[768,128]{1,0:T(8,128)S(1)} %constant_dynamic-update-slice_fusion.packed_ref, f32[384,128]{1,0:T(8,128)S(1)} %copy-done.8), custom_call_target="tpu_custom_call" | custom-call | tf_op jit(solution)/shard_map/leading_basis/pallas_call | solution.py:86
  152.9 1.8 %project_x.1 = f32[16,3,32,128]{3,2,1,0:T(8,128)} custom-call(f32[384,1536]{1,0:T(8,128)S(1)} %get-tuple-element.14.cols_ref, f32[128,384]{1,0:T(8,128)S(1)} %leading_basis.3.basis_ref), custom_call_target="tpu_custom_call" | custom-call | tf_op jit(solution)/shard_map/project_x/pallas_call | solution.py:270
  (72 shorter events, 31.5 us)
Async XLA Ops:
  10.4 1.8 %collective-permute-start = (f32[640,128]{1,0:T(8,128)S(1)}, f32[640,128]{1,0:T(8,128)S(1)}, u32[]{:S(2)}, u32[]{:S(2)}) collective-permute-start(f32[640,128]{1,0:T(8,128)S(1)} %constant_dynamic-slice_fusion.7), channel_id=1, source_target_pairs={{0,8},{1,9},{2,10},{3,11},{4,12},{5,13},{6,14},{7,15},{8,0},{9,1},... | collective-permute-start | bytes 983048 | tf_op jit(solution)/shard_map/ppermute | solution.py:292
  12.2 28.1 %copy-start.7 = (f32[512,128]{1,0:T(8,128)S(1)}, f32[512,128]{1,0:T(8,128)}, u32[]{:S(2)}) copy-start(f32[512,128]{1,0:T(8,128)} %sketch_ref.2) | copy-start | bytes 786436
  12.3 6.7 %collective-permute-start.3 = (f32[160,128]{1,0:T(8,128)S(1)}, f32[160,128]{1,0:T(8,128)S(1)}, u32[]{:S(2)}, u32[]{:S(2)}) collective-permute-start(f32[160,128]{1,0:T(8,128)S(1)} %get-tuple-element.21), channel_id=1, source_target_pairs={{0,17},{1,16},{2,19},{3,18},{4,21},{5,20},{6,23},{7,22},{8,25},{9,... | collective-permute-start | bytes 245768 | tf_op jit(solution)/shard_map/ppermute | solution.py:292
  16.1 4.5 %collective-permute-start.2 = (f32[160,128]{1,0:T(8,128)S(1)}, f32[160,128]{1,0:T(8,128)S(1)}, u32[]{:S(2)}, u32[]{:S(2)}) collective-permute-start(f32[160,128]{1,0:T(8,128)S(1)} %get-tuple-element.22), channel_id=1, source_target_pairs={{0,16},{1,17},{2,18},{3,19},{4,20},{5,21},{6,22},{7,23},{8,24},{9,... | collective-permute-start | bytes 245768 | tf_op jit(solution)/shard_map/ppermute | solution.py:292
  16.7 4.4 %collective-permute-start.1 = (f32[160,128]{1,0:T(8,128)S(1)}, f32[160,128]{1,0:T(8,128)S(1)}, u32[]{:S(2)}, u32[]{:S(2)}) collective-permute-start(f32[160,128]{1,0:T(8,128)S(1)} %get-tuple-element.20), channel_id=1, source_target_pairs={{0,1},{1,0},{2,3},{3,2},{4,5},{5,4},{6,7},{7,6},{8,9},{9,8},{10,11... | collective-permute-start | bytes 245768 | tf_op jit(solution)/shard_map/ppermute | solution.py:292
  21.1 4.5 %collective-permute-start.4 = (f32[160,128]{1,0:T(8,128)S(1)}, f32[160,128]{1,0:T(8,128)S(1)}, u32[]{:S(2)}, u32[]{:S(2)}) collective-permute-start(f32[160,128]{1,0:T(8,128)S(1)} %add_add_fusion), channel_id=1, source_target_pairs={{0,2},{1,3},{2,0},{3,1},{4,6},{5,7},{6,4},{7,5},{8,10},{9,11},{10,... | collective-permute-start | bytes 245768 | tf_op jit(solution)/shard_map/ppermute | solution.py:292
  25.6 5.4 %collective-permute-start.5 = (f32[160,128]{1,0:T(8,128)S(1)}, f32[160,128]{1,0:T(8,128)S(1)}, u32[]{:S(2)}, u32[]{:S(2)}) collective-permute-start(f32[160,128]{1,0:T(8,128)S(1)} %add.104), channel_id=1, source_target_pairs={{0,4},{1,5},{2,6},{3,7},{4,0},{5,1},{6,2},{7,3},{8,12},{9,13},{10,... | collective-permute-start | bytes 245768 | tf_op jit(solution)/shard_map/ppermute | solution.py:292
  31.1 4.5 %collective-permute-start.6 = (f32[160,128]{1,0:T(8,128)S(1)}, f32[160,128]{1,0:T(8,128)S(1)}, u32[]{:S(2)}, u32[]{:S(2)}) collective-permute-start(f32[160,128]{1,0:T(8,128)S(1)} %get-tuple-element.19), channel_id=1, source_target_pairs={{0,1},{1,0},{2,3},{3,2},{4,5},{5,4},{6,7},{7,6},{8,9},{9,8},{10,11... | collective-permute-start | bytes 245768 | tf_op jit(solution)/shard_map/ppermute | solution.py:292
  32.5 4.4 %collective-permute-start.7 = (f32[160,128]{1,0:T(8,128)S(1)}, f32[160,128]{1,0:T(8,128)S(1)}, u32[]{:S(2)}, u32[]{:S(2)}) collective-permute-start(f32[160,128]{1,0:T(8,128)S(1)} %get-tuple-element.19), channel_id=1, source_target_pairs={{0,16},{1,17},{2,18},{3,19},{4,20},{5,21},{6,22},{7,23},{8,24},{9,... | collective-permute-start | bytes 245768 | tf_op jit(solution)/shard_map/ppermute | solution.py:292
  33.2 5.3 %collective-permute-start.8 = (f32[160,128]{1,0:T(8,128)S(1)}, f32[160,128]{1,0:T(8,128)S(1)}, u32[]{:S(2)}, u32[]{:S(2)}) collective-permute-start(f32[160,128]{1,0:T(8,128)S(1)} %get-tuple-element.19), channel_id=1, source_target_pairs={{0,17},{1,16},{2,19},{3,18},{4,21},{5,20},{6,23},{7,22},{8,25},{9,... | collective-permute-start | bytes 245768 | tf_op jit(solution)/shard_map/ppermute | solution.py:292
  38.6 1.7 %collective-permute-start.9 = (f32[640,128]{1,0:T(8,128)S(1)}, f32[640,128]{1,0:T(8,128)S(1)}, u32[]{:S(2)}, u32[]{:S(2)}) collective-permute-start(f32[640,128]{1,0:T(8,128)S(1)} %constant_dynamic-update-slice_fusion.8), channel_id=1, source_target_pairs={{0,8},{1,9},{2,10},{3,11},{4,12},{5,13},{6,14},{7,15},{8,0},{9,1},... | collective-permute-start | bytes 983048 | tf_op jit(solution)/shard_map/ppermute | solution.py:292
  71.7 2.2 %collective-permute-start.10 = (f32[96,1536]{1,0:T(8,128)}, f32[96,1536]{1,0:T(8,128)S(1)}, u32[]{:S(2)}, u32[]{:S(2)}) collective-permute-start(f32[96,1536]{1,0:T(8,128)} %get-tuple-element.11), channel_id=1, source_target_pairs={{0,8},{1,9},{2,10},{3,11},{4,12},{5,13},{6,14},{7,15},{8,0},{9,1},... | collective-permute-start | bytes 1769480 | tf_op jit(solution)/shard_map/ppermute | solution.py:292
  71.8 16.1 %collective-permute-start.11 = (f32[96,1536]{1,0:T(8,128)S(1)}, f32[96,1536]{1,0:T(8,128)S(1)}, u32[]{:S(2)}, u32[]{:S(2)}) collective-permute-start(f32[96,1536]{1,0:T(8,128)S(1)} %get-tuple-element.12), channel_id=1, source_target_pairs={{0,16},{1,17},{2,18},{3,19},{4,20},{5,21},{6,22},{7,23},{8,24},{9,... | collective-permute-start | bytes 1769480 | tf_op jit(solution)/shard_map/ppermute | solution.py:292
  73.2 26.2 %collective-permute-start.12 = (f32[96,1536]{1,0:T(8,128)S(1)}, f32[96,1536]{1,0:T(8,128)S(1)}, u32[]{:S(2)}, u32[]{:S(2)}) collective-permute-start(f32[96,1536]{1,0:T(8,128)S(1)} %get-tuple-element.13), channel_id=1, source_target_pairs={{0,24},{1,25},{2,26},{3,27},{4,28},{5,29},{6,30},{7,31},{8,16},{9,... | collective-permute-start | bytes 1769480 | tf_op jit(solution)/shard_map/ppermute | solution.py:292
  105.2 1.5 collective-permute-start.13
  107.7 5.1 %collective-permute-start.16 = (f32[96,128]{1,0:T(8,128)S(1)}, f32[96,128]{1,0:T(8,128)S(1)}, u32[]{:S(2)}, u32[]{:S(2)}) collective-permute-start(f32[96,128]{1,0:T(8,128)S(1)} %get-tuple-element.24), channel_id=1, source_target_pairs={{0,17},{1,16},{2,19},{3,18},{4,21},{5,20},{6,23},{7,22},{8,25},{9,... | collective-permute-start | bytes 147464 | tf_op jit(solution)/shard_map/ppermute | solution.py:292
  109.3 4.5 %collective-permute-start.15 = (f32[96,128]{1,0:T(8,128)S(1)}, f32[96,128]{1,0:T(8,128)S(1)}, u32[]{:S(2)}, u32[]{:S(2)}) collective-permute-start(f32[96,128]{1,0:T(8,128)S(1)} %get-tuple-element.25), channel_id=1, source_target_pairs={{0,16},{1,17},{2,18},{3,19},{4,20},{5,21},{6,22},{7,23},{8,24},{9,... | collective-permute-start | bytes 147464 | tf_op jit(solution)/shard_map/ppermute | solution.py:292
  110.8 4.1 %collective-permute-start.14 = (f32[96,128]{1,0:T(8,128)S(1)}, f32[96,128]{1,0:T(8,128)S(1)}, u32[]{:S(2)}, u32[]{:S(2)}) collective-permute-start(f32[96,128]{1,0:T(8,128)S(1)} %get-tuple-element.23), channel_id=1, source_target_pairs={{0,1},{1,0},{2,3},{3,2},{4,5},{5,4},{6,7},{7,6},{8,9},{9,8},{10,11... | collective-permute-start | bytes 147464 | tf_op jit(solution)/shard_map/ppermute | solution.py:292
  114.9 4.2 %collective-permute-start.17 = (f32[96,128]{1,0:T(8,128)S(1)}, f32[96,128]{1,0:T(8,128)S(1)}, u32[]{:S(2)}, u32[]{:S(2)}) collective-permute-start(f32[96,128]{1,0:T(8,128)S(1)} %add_add_fusion.1), channel_id=1, source_target_pairs={{0,2},{1,3},{2,0},{3,1},{4,6},{5,7},{6,4},{7,5},{8,10},{9,11},{10,... | collective-permute-start | bytes 147464 | tf_op jit(solution)/shard_map/ppermute | solution.py:292
  119.0 5.0 %collective-permute-start.18 = (f32[96,128]{1,0:T(8,128)S(1)}, f32[96,128]{1,0:T(8,128)S(1)}, u32[]{:S(2)}, u32[]{:S(2)}) collective-permute-start(f32[96,128]{1,0:T(8,128)S(1)} %add.116), channel_id=1, source_target_pairs={{0,4},{1,5},{2,6},{3,7},{4,0},{5,1},{6,2},{7,3},{8,12},{9,13},{10,... | collective-permute-start | bytes 147464 | tf_op jit(solution)/shard_map/ppermute | solution.py:292
  124.1 4.2 %collective-permute-start.19 = (f32[96,128]{1,0:T(8,128)S(1)}, f32[96,128]{1,0:T(8,128)S(1)}, u32[]{:S(2)}, u32[]{:S(2)}) collective-permute-start(f32[96,128]{1,0:T(8,128)S(1)} %get-tuple-element.17), channel_id=1, source_target_pairs={{0,1},{1,0},{2,3},{3,2},{4,5},{5,4},{6,7},{7,6},{8,9},{9,8},{10,11... | collective-permute-start | bytes 147464 | tf_op jit(solution)/shard_map/ppermute | solution.py:292
  124.7 4.1 %collective-permute-start.20 = (f32[96,128]{1,0:T(8,128)S(1)}, f32[96,128]{1,0:T(8,128)S(1)}, u32[]{:S(2)}, u32[]{:S(2)}) collective-permute-start(f32[96,128]{1,0:T(8,128)S(1)} %get-tuple-element.17), channel_id=1, source_target_pairs={{0,16},{1,17},{2,18},{3,19},{4,20},{5,21},{6,22},{7,23},{8,24},{9,... | collective-permute-start | bytes 147464 | tf_op jit(solution)/shard_map/ppermute | solution.py:292
  126.0 5.0 %collective-permute-start.21 = (f32[96,128]{1,0:T(8,128)S(1)}, f32[96,128]{1,0:T(8,128)S(1)}, u32[]{:S(2)}, u32[]{:S(2)}) collective-permute-start(f32[96,128]{1,0:T(8,128)S(1)} %get-tuple-element.17), channel_id=1, source_target_pairs={{0,17},{1,16},{2,19},{3,18},{4,21},{5,20},{6,23},{7,22},{8,25},{9,... | collective-permute-start | bytes 147464 | tf_op jit(solution)/shard_map/ppermute | solution.py:292
  131.0 1.4 collective-permute-start.22
  (8 other events, 39.9 us)
